TPU v7x, 32 devices: a whole 2x2x4 slice. The times are simulated.
32 devices in a mesh: sx: 4 (over z), sy: 4 (over y, core), ev: 2 (over x).
Axes of the slice: x: 2, y: 2, z: 4, core: 2. Of those that a mesh axis runs over, the one named last changes fastest.
Arguments:
- adjoint_state: float32 [2, 9, 32, 32, 128], P('ev', None, 'sx', 'sy'), may hold values from -6 to 6
- forward_state: bfloat16 [2, 3, 9, 32, 32, 128], P('ev', None, None, 'sx', 'sy'), may hold values from -6 to 6
- inv_density: float32 [32, 32, 128], P('sx', 'sy'), may hold values from 0.6 to 1.6
- lame_lambda: float32 [32, 32, 128], P('sx', 'sy'), may hold values from 0.15 to 0.5
- shear_modulus: float32 [32, 32, 128], P('sx', 'sy'), may hold values from 0.1 to 0.4
- station_block: int32 [2, 512, 1], P('ev', ('sx', 'sy')), may hold values from 0 to 3; in each aligned block of 32 rows (0 to 31, 32 to 63, ..., all dimensions but the last counted through in order) at most 16 rows name the same one
- station_cell: int32 [2, 512], P('ev', ('sx', 'sy')), may hold values from 0 to 63
- station_trace: float32 [2, 512, 9], P('ev', ('sx', 'sy')), may hold values from -6 to 6
- source_count: int32 [2, 16], P('ev', ('sx', 'sy')), may hold values from 1 to 32, 392 in all within a row
Outputs:
- adjoint_final: float32 [2, 9, 32, 32, 128], P('ev', None, 'sx', 'sy')
- kernels: float32 [3, 32, 32, 128], P(None, 'sx', 'sy')
Inputs may be any that keep to these rules, and one draw needn't show every extreme that they name: `station_block`: among the 32 rows of one device no block is named more than 16 times.
All inputs are finite; a program needn't handle non-finite values. No bound on the sum of `source_count` on one device may be relied on, other than what follows from the above.
Results may differ from a plain program's by a relative error of at most 0.0003.
Values sent between devices are 32-bit elements; how exact they have to be, the bound alone decides.
A program may use at most 64 MiB of HBM per device.

v0:
```python
import jax
import jax.numpy as jnp
from jax import lax
from jax.sharding import PartitionSpec as P

DT = 0.35
stress_faces = ([0], [3, 4], [1], [3, 5])
velocity_faces = ([1, 2], [0], [0, 2], [1])


def passed_along(value, axis, steps):
    count = lax.axis_size(axis)
    leading, last = (max(0, -steps), min(count, count - steps))
    return lax.ppermute(value, axis, [(source, source + steps) for source in range(leading, last)])


def shift_upper(field, axis, plane):
    size = field.shape[axis]
    inner = lax.slice_in_dim(field, 1, size, axis=axis)
    return jnp.concatenate([inner, plane], axis=axis)


def shift_lower(field, axis, plane):
    size = field.shape[axis]
    inner = lax.slice_in_dim(field, 0, size - 1, axis=axis)
    return jnp.concatenate([plane, inner], axis=axis)


def above_diff(field):
    zeros_plane = jnp.zeros(field.shape[:-1] + (1,), jnp.float32)
    return jnp.concatenate([field[..., 1:], zeros_plane], axis=-1) - field


def below_diff(field):
    zeros_plane = jnp.zeros(field.shape[:-1] + (1,), jnp.float32)
    return field - jnp.concatenate([zeros_plane, field[..., :-1]], axis=-1)


def accelerate(stress, planes, inv_density, force):
    high_x, low_x, high_y, low_y = planes
    next_x = shift_upper(stress[:, stress_faces[0]], 2, high_x)
    prev_x = shift_lower(stress[:, stress_faces[1]], 2, low_x)
    next_y = shift_upper(stress[:, stress_faces[2]], 3, high_y)
    prev_y = shift_lower(stress[:, stress_faces[3]], 3, low_y)
    sxx, syy, szz, sxy, sxz, syz = [stress[:, c] for c in range(6)]
    accel_x = next_x[:, 0] - sxx + (sxy - prev_y[:, 0]) + below_diff(sxz)
    accel_y = sxy - prev_x[:, 0] + (next_y[:, 0] - syy) + below_diff(syz)
    accel_z = sxz - prev_x[:, 1] + (syz - prev_y[:, 1]) + above_diff(szz)
    accel = jnp.stack([accel_x, accel_y, accel_z], axis=1)
    accel = accel.at[..., 0].add(force)
    return DT * inv_density * accel


def strain_rates(velocity, planes):
    high_x, low_x, high_y, low_y = planes
    next_x = shift_upper(velocity[:, velocity_faces[0]], 2, high_x)
    prev_x = shift_lower(velocity[:, velocity_faces[1]], 2, low_x)
    next_y = shift_upper(velocity[:, velocity_faces[2]], 3, high_y)
    prev_y = shift_lower(velocity[:, velocity_faces[3]], 3, low_y)
    vel_x, vel_y, vel_z = (velocity[:, 0], velocity[:, 1], velocity[:, 2])
    rate_xx = vel_x - prev_x[:, 0]
    rate_yy = vel_y - prev_y[:, 0]
    rate_zz = below_diff(vel_z)
    rate_xy = 0.5 * (next_y[:, 0] - vel_x + (next_x[:, 0] - vel_y))
    rate_xz = 0.5 * (above_diff(vel_x) + (next_x[:, 1] - vel_z))
    rate_yz = 0.5 * (above_diff(vel_y) + (next_y[:, 1] - vel_z))
    return jnp.stack([rate_xx, rate_yy, rate_zz, rate_xy, rate_xz, rate_yz], axis=1)


def stress_step(stress, rates, lame_lambda, shear_modulus):
    trace = rates[:, 0] + rates[:, 1] + rates[:, 2]
    diagonal = stress[:, :3] + DT * (
        lame_lambda * trace[:, None] + 2.0 * shear_modulus * rates[:, :3]
    )
    offdiag = stress[:, 3:] + DT * 2.0 * shear_modulus * rates[:, 3:]
    return jnp.concatenate([diagonal, offdiag], axis=1)


def kernel_terms(rates, strains):
    trace = rates[:, 0] + rates[:, 1] + rates[:, 2]
    forward_trace = strains[:, 0] + strains[:, 1] + strains[:, 2]
    lambda_term = DT * forward_trace * trace
    shear_term = (
        DT
        * 2.0
        * (
            jnp.sum(strains[:, :3] * rates[:, :3], axis=1)
            + 2.0 * jnp.sum(strains[:, 3:] * rates[:, 3:], axis=1)
        )
    )
    return (lambda_term, shear_term)


def border_planes(stack, faces):
    high_x = passed_along(stack[:, faces[0], :1], "sx", -1)
    low_x = passed_along(stack[:, faces[1], -1:], "sx", 1)
    high_y = passed_along(stack[:, faces[2], :, :1], "sy", -1)
    low_y = passed_along(stack[:, faces[3], :, -1:], "sy", 1)
    return (high_x, low_x, high_y, low_y)


def pack_rows(position, values, cells, slots):
    send_values = jnp.zeros((slots, values.shape[1]), jnp.float32).at[position].set(values)
    send_cells = jnp.zeros((slots,), jnp.float32).at[position].set(cells.astype(jnp.float32))
    return (send_values, send_cells)


def on_device(
    adjoint_state,
    forward_state,
    inv_density,
    lame_lambda,
    shear_modulus,
    station_block,
    station_cell,
    station_trace,
    source_count,
):
    events, owned = station_cell.shape
    blocks_y = lax.axis_size("sy")
    capacity = max(2, 2 * owned // blocks_y)
    slots = blocks_y * capacity
    width_x, width_y = (adjoint_state.shape[2], adjoint_state.shape[3])
    steps = forward_state.shape[1]
    live = (jnp.arange(owned, dtype=jnp.int32)[None, :] < source_count).astype(jnp.float32)
    traces = station_trace * live[:, :, None]
    targets = station_block[:, :, 0]
    member = (targets[:, :, None] == jnp.arange(blocks_y, dtype=jnp.int32)[None, None, :]).astype(
        jnp.int32
    )
    earlier = jnp.cumsum(member, axis=1) - member
    rank = jnp.sum(earlier * member, axis=2)
    position = targets * capacity + rank
    send_values, send_cells = jax.vmap(lambda pos, vals, cells: pack_rows(pos, vals, cells, slots))(
        position, traces, station_cell
    )
    surface_ids = jnp.arange(width_x * width_y, dtype=jnp.float32)
    zero_k = jnp.zeros((events,) + adjoint_state.shape[2:], jnp.float32)
    rho_kernel, lambda_kernel, shear_kernel = (zero_k, zero_k, zero_k)
    state = adjoint_state
    for step in range(steps):
        step_values = lax.all_to_all(
            send_values[:, :, 3 * step : 3 * step + 3],
            "sy",
            split_axis=1,
            concat_axis=1,
            tiled=True,
        )
        step_cells = lax.all_to_all(send_cells, "sy", split_axis=1, concat_axis=1, tiled=True)
        table = (surface_ids[None, :, None] == step_cells[:, None, :]).astype(jnp.float32)
        dense = jnp.einsum("ecr,erw->ecw", table, step_values, precision=lax.Precision.HIGHEST)
        here = dense.reshape(events, width_x, width_y, step_values.shape[2])
        force = jnp.moveaxis(here, 3, 1)
        stress = state[:, 3:]
        change = accelerate(stress, border_planes(stress, stress_faces), inv_density, force)
        velocity = state[:, :3] + change
        rho_kernel = rho_kernel + jnp.sum(
            forward_state[:, step, :3].astype(jnp.float32) * change, axis=1
        )
        rates = strain_rates(velocity, border_planes(velocity, velocity_faces))
        stress = stress_step(stress, rates, lame_lambda, shear_modulus)
        lambda_term, shear_term = kernel_terms(
            rates, forward_state[:, step, 3:].astype(jnp.float32)
        )
        lambda_kernel = lambda_kernel + lambda_term
        shear_kernel = shear_kernel + shear_term
        state = jnp.concatenate([velocity, stress], axis=1)
    totals = lax.psum(
        (
            jnp.sum(rho_kernel, axis=0),
            jnp.sum(lambda_kernel, axis=0),
            jnp.sum(shear_kernel, axis=0),
        ),
        "ev",
    )
    return (state, jnp.stack(totals, axis=0))


def solution(mesh):
    return jax.shard_map(
        on_device,
        mesh=mesh,
        in_specs=(
            P("ev", None, "sx", "sy", None),
            P("ev", None, None, "sx", "sy", None),
            P("sx", "sy", None),
            P("sx", "sy", None),
            P("sx", "sy", None),
            P("ev", ("sx", "sy"), None),
            P("ev", ("sx", "sy")),
            P("ev", ("sx", "sy"), None),
            P("ev", ("sx", "sy")),
        ),
        out_specs=(P("ev", None, "sx", "sy", None), P(None, "sx", "sy", None)),
        check_vma=False,
    )
```

profile of v0, /device:TPU:0, one launch (start us, length us, event | category | flops | bytes accessed | tf_op | source)
XLA Modules:
  0.0 155.8 jit_solution(4922880001029107132)
XLA Ops:
  7.2 0.8 slice.986
  7.9 1.4 collective-permute-start.3
  9.3 0.7 slice.983
  10.0 1.3 collective-permute-start
  11.4 0.6 copy-done.9
  12.4 0.7 scatter_custom_fusion
  13.0 0.7 all_to_all.17
  13.7 5.0 %all-to-all-start = ((f32[1,4,16]{2,0,1:T(1,128)}), f32[1,4,16]{2,0,1:T(1,128)S(1)}, u32[]{:S(2)}, u32[]{:S(2)}) async-start(f32[1,4,16]{2,0,1:T(1,128)} %bitcast.23), calls=%async_computation | async-start | bytes 4096 | tf_op jit(solution)/shard_map/all_to_all | solution.py:149
  18.7 1.0 fusion.161
  19.7 0.6 gather_fusion.2
  20.3 4.4 %collective-permute-start.2 = (f32[1,2,1,8,128]{4,3,1,2,0:T(8,128)S(1)}, f32[1,2,1,8,128]{4,3,1,2,0:T(8,128)S(1)}, u32[]{:S(2)}, u32[]{:S(2)}) collective-permute-start(f32[1,2,1,8,128]{4,3,1,2,0:T(8,128)S(1)} %bitcast.607), channel_id=1, source_target_pairs={{0,8},{8,16},{16,24},{1,9},{9,17},{17,25},{2,10},{10,18},{18,26},{... | collective-permute-start | bytes 24584 | tf_op jit(solution)/shard_map/ppermute | solution.py:14
  24.8 0.6 gather_fusion
  25.4 2.1 %collective-permute-start.1 = (f32[1,2,8,1,128]{4,2,3,1,0:T(8,128)S(1)}, f32[1,2,8,1,128]{4,2,3,1,0:T(8,128)S(1)}, u32[]{:S(2)}, u32[]{:S(2)}) collective-permute-start(f32[1,2,8,1,128]{4,2,3,1,0:T(8,128)S(1)} %bitcast.606), channel_id=1, source_target_pairs={{0,2},{2,4},{4,6},{1,3},{3,5},{5,7},{8,10},{10,12},{12,14},{9,11},... | collective-permute-start | bytes 24584 | tf_op jit(solution)/shard_map/ppermute | solution.py:14
  28.4 0.7 scatter_custom_fusion.1
  29.1 0.7 fusion.162
  30.2 0.6 gather_fusion.1
  30.7 0.6 gather_fusion.3
  31.3 3.3 %all-to-all-start.1 = ((f32[1,64,3]{2,0,1:T(1,128)}), f32[1,64,3]{2,0,1:T(1,128)S(1)}, u32[]{:S(2)}, u32[]{:S(2)}) async-start(f32[1,64,3]{2,0,1:T(1,128)} %bitcast.28), calls=%async_computation.1 | async-start | bytes 65536 | tf_op jit(solution)/shard_map/all_to_all | solution.py:142
  35.1 0.6 reduce.19
  36.3 2.2 %all-to-all-done.1 = f32[1,64,3]{2,0,1:T(1,128)S(1)} async-done(((f32[1,64,3]{2,0,1:T(1,128)}), f32[1,64,3]{2,0,1:T(1,128)S(1)}, u32[]{:S(2)}, u32[]{:S(2)}) %all-to-all-start.1) | async-done | bytes 800 | tf_op jit(solution)/shard_map/all_to_all | solution.py:142
  38.5 3.3 %all-to-all-start.2 = ((f32[1,64,3]{2,0,1:T(1,128)}), f32[1,64,3]{2,0,1:T(1,128)S(1)}, u32[]{:S(2)}, u32[]{:S(2)}) async-start(f32[1,64,3]{2,0,1:T(1,128)} %bitcast.72), calls=%async_computation.2 | async-start | bytes 65536 | tf_op jit(solution)/shard_map/all_to_all | solution.py:142
  43.2 3.6 %collective-permute-start.4 = (f32[1,1,1,8,128]{4,3,2,1,0:T(8,128)S(1)}, f32[1,1,1,8,128]{4,3,2,1,0:T(8,128)S(1)}, u32[]{:S(2)}, u32[]{:S(2)}) collective-permute-start(f32[1,1,1,8,128]{4,3,2,1,0:T(8,128)S(1)} %slice.1093), channel_id=1, source_target_pairs={{0,8},{8,16},{16,24},{1,9},{9,17},{17,25},{2,10},{10,18},{18,26},{... | collective-permute-start | bytes 12296 | tf_op jit(solution)/shard_map/ppermute | solution.py:14
  46.8 2.1 %collective-permute-start.5 = (f32[1,1,8,1,128]{4,3,2,1,0:T(1,128)S(1)}, f32[1,1,8,1,128]{4,3,2,1,0:T(1,128)S(1)}, u32[]{:S(2)}, u32[]{:S(2)}) collective-permute-start(f32[1,1,8,1,128]{4,3,2,1,0:T(1,128)S(1)} %slice.1096), channel_id=1, source_target_pairs={{0,2},{2,4},{4,6},{1,3},{3,5},{5,7},{8,10},{10,12},{12,14},{9,11},... | collective-permute-start | bytes 12296 | tf_op jit(solution)/shard_map/ppermute | solution.py:14
  48.9 1.3 collective-permute-start.7
  50.7 1.3 collective-permute-start.6
  52.1 0.6 gather_fusion.6
  52.6 0.6 gather_fusion.4
  53.2 1.2 collective-permute-done.7
  54.4 0.8 collective-permute-done.6
  55.5 0.7 copy-done.2
  56.4 1.3 collective-permute-start.11
  57.7 0.6 gather_fusion.10
  58.2 4.3 %collective-permute-start.10 = (f32[1,2,1,8,128]{4,3,1,2,0:T(8,128)S(1)}, f32[1,2,1,8,128]{4,3,1,2,0:T(8,128)S(1)}, u32[]{:S(2)}, u32[]{:S(2)}) collective-permute-start(f32[1,2,1,8,128]{4,3,1,2,0:T(8,128)S(1)} %bitcast.614), channel_id=1, source_target_pairs={{0,8},{8,16},{16,24},{1,9},{9,17},{17,25},{2,10},{10,18},{18,26},{... | collective-permute-start | bytes 24584 | tf_op jit(solution)/shard_map/ppermute | solution.py:14
  62.6 0.6 gather_fusion.8
  64.3 1.3 collective-permute-start.8
  65.7 4.6 %collective-permute-start.9 = (f32[1,2,8,1,128]{4,2,3,1,0:T(8,128)S(1)}, f32[1,2,8,1,128]{4,2,3,1,0:T(8,128)S(1)}, u32[]{:S(2)}, u32[]{:S(2)}) collective-permute-start(f32[1,2,8,1,128]{4,2,3,1,0:T(8,128)S(1)} %bitcast.615), channel_id=1, source_target_pairs={{0,2},{2,4},{4,6},{1,3},{3,5},{5,7},{8,10},{10,12},{12,14},{9,11},... | collective-permute-start | bytes 24584 | tf_op jit(solution)/shard_map/ppermute | solution.py:14
  70.5 0.6 collective-permute-done.9
  72.9 1.3 collective-permute-start.15
  74.2 0.6 gather_fusion.13
  74.7 1.3 collective-permute-start.14
  76.1 4.9 %collective-permute-start.12 = (f32[1,1,1,8,128]{4,3,2,1,0:T(8,128)S(1)}, f32[1,1,1,8,128]{4,3,2,1,0:T(8,128)S(1)}, u32[]{:S(2)}, u32[]{:S(2)}) collective-permute-start(f32[1,1,1,8,128]{4,3,2,1,0:T(8,128)S(1)} %slice.1130), channel_id=1, source_target_pairs={{0,8},{8,16},{16,24},{1,9},{9,17},{17,25},{2,10},{10,18},{18,26},{... | collective-permute-start | bytes 12296 | tf_op jit(solution)/shard_map/ppermute | solution.py:14
  81.0 4.5 %collective-permute-start.13 = (f32[1,1,8,1,128]{4,3,2,1,0:T(1,128)S(1)}, f32[1,1,8,1,128]{4,3,2,1,0:T(1,128)S(1)}, u32[]{:S(2)}, u32[]{:S(2)}) collective-permute-start(f32[1,1,8,1,128]{4,3,2,1,0:T(1,128)S(1)} %slice.1133), channel_id=1, source_target_pairs={{0,2},{2,4},{4,6},{1,3},{3,5},{5,7},{8,10},{10,12},{12,14},{9,11},... | collective-permute-start | bytes 12296 | tf_op jit(solution)/shard_map/ppermute | solution.py:14
  85.5 3.9 %all-to-all-start.3 = ((f32[1,64,3]{2,0,1:T(1,128)}), f32[1,64,3]{2,0,1:T(1,128)S(1)}, u32[]{:S(2)}, u32[]{:S(2)}) async-start(f32[1,64,3]{2,0,1:T(1,128)} %bitcast.116), calls=%async_computation.3 | async-start | bytes 65536 | tf_op jit(solution)/shard_map/all_to_all | solution.py:142
  91.1 1.3 collective-permute-start.19
  93.0 3.9 %collective-permute-start.18 = (f32[1,2,1,8,128]{4,3,1,2,0:T(8,128)S(1)}, f32[1,2,1,8,128]{4,3,1,2,0:T(8,128)S(1)}, u32[]{:S(2)}, u32[]{:S(2)}) collective-permute-start(f32[1,2,1,8,128]{4,3,1,2,0:T(8,128)S(1)} %bitcast.611), channel_id=1, source_target_pairs={{0,8},{8,16},{16,24},{1,9},{9,17},{17,25},{2,10},{10,18},{18,26},{... | collective-permute-start | bytes 24584 | tf_op jit(solution)/shard_map/ppermute | solution.py:14
  97.0 0.6 gather_fusion.16
  97.6 0.6 gather_fusion.19
  98.7 1.3 collective-permute-start.16
  100.1 4.2 %collective-permute-start.17 = (f32[1,2,8,1,128]{4,2,3,1,0:T(8,128)S(1)}, f32[1,2,8,1,128]{4,2,3,1,0:T(8,128)S(1)}, u32[]{:S(2)}, u32[]{:S(2)}) collective-permute-start(f32[1,2,8,1,128]{4,2,3,1,0:T(8,128)S(1)} %bitcast.612), channel_id=1, source_target_pairs={{0,2},{2,4},{4,6},{1,3},{3,5},{5,7},{8,10},{10,12},{12,14},{9,11},... | collective-permute-start | bytes 24584 | tf_op jit(solution)/shard_map/ppermute | solution.py:14
  104.4 0.6 collective-permute-done.17
  106.3 0.6 gather_fusion.23
  106.9 4.3 %collective-permute-start.20 = (f32[1,1,1,8,128]{4,3,2,1,0:T(8,128)S(1)}, f32[1,1,1,8,128]{4,3,2,1,0:T(8,128)S(1)}, u32[]{:S(2)}, u32[]{:S(2)}) collective-permute-start(f32[1,1,1,8,128]{4,3,2,1,0:T(8,128)S(1)} %slice.1167), channel_id=1, source_target_pairs={{0,8},{8,16},{16,24},{1,9},{9,17},{17,25},{2,10},{10,18},{18,26},{... | collective-permute-start | bytes 12296 | tf_op jit(solution)/shard_map/ppermute | solution.py:14
  111.2 3.9 %collective-permute-start.21 = (f32[1,1,8,1,128]{4,3,2,1,0:T(1,128)S(1)}, f32[1,1,8,1,128]{4,3,2,1,0:T(1,128)S(1)}, u32[]{:S(2)}, u32[]{:S(2)}) collective-permute-start(f32[1,1,8,1,128]{4,3,2,1,0:T(1,128)S(1)} %slice.1170), channel_id=1, source_target_pairs={{0,2},{2,4},{4,6},{1,3},{3,5},{5,7},{8,10},{10,12},{12,14},{9,11},... | collective-permute-start | bytes 12296 | tf_op jit(solution)/shard_map/ppermute | solution.py:14
  115.1 1.3 collective-permute-start.23
  116.9 1.3 collective-permute-start.22
  118.2 0.6 add_bitcast_fusion
  119.4 0.6 gather_fusion.20
  120.0 0.6 collective-permute-done.23
  120.6 1.5 collective-permute-done.22
  122.1 0.7 fusion.69
  123.1 0.6 multiply_bitcast_fusion
  123.7 0.7 pad_maximum_fusion
  124.5 23.1 %all-reduce.33.cloned.1.call-done = (f32[1,8,8,128]{3,2,1,0:T(8,128)}, f32[1,8,8,128]{3,2,1,0:T(8,128)}, f32[1,8,8,128]{3,2,1,0:T(8,128)}) async-done(((f32[1,8,8,128]{3,2,1,0:T(8,128)}, f32[1,8,8,128]{3,2,1,0:T(8,128)}, f32[1,8,8,128]{3,2,1,0:T(8,128)}), (f32[1,8,8,128]{3,2,1,0:T(8,128)}, f32[1,8,8,128]{3,2,1,0:T(8,128)}, f32[1,8,8,128]{3,2,1,0:T(8,128)})) %all-reduce.33.cloned.1.call-update) | async-done | bytes 98320 | tf_op jit(solution)/shard_map/psum | solution.py:168
  147.5 1.4 pad_maximum_fusion.12
  (174 shorter events, 13.0 us)
Async XLA Ops:
  7.9 3.4 %copy-start.12 = (s32[1,32]{1,0:T(1,128)S(1)}, s32[1,32]{1,0:T(1,128)}, u32[]{:S(2)}) copy-start(s32[1,32]{1,0:T(1,128)} %param.69) | copy-start | bytes 388
  7.9 27.9 %collective-permute-start.3 = (f32[1,1,8,1,128]{4,3,2,1,0:T(1,128)S(1)}, f32[1,1,8,1,128]{4,3,2,1,0:T(1,128)S(1)}, u32[]{:S(2)}, u32[]{:S(2)}) collective-permute-start(f32[1,1,8,1,128]{4,3,2,1,0:T(1,128)S(1)} %slice.986), channel_id=1, source_target_pairs={{2,0},{4,2},{6,4},{3,1},{5,3},{7,5},{10,8},{12,10},{14,12},{11,9},... | collective-permute-start | bytes 12296 | tf_op jit(solution)/shard_map/ppermute | solution.py:14
  10.0 25.9 %collective-permute-start = (f32[1,1,1,8,128]{4,3,2,1,0:T(8,128)S(1)}, f32[1,1,1,8,128]{4,3,2,1,0:T(8,128)S(1)}, u32[]{:S(2)}, u32[]{:S(2)}) collective-permute-start(f32[1,1,1,8,128]{4,3,2,1,0:T(8,128)S(1)} %slice.983), channel_id=1, source_target_pairs={{8,0},{16,8},{24,16},{9,1},{17,9},{25,17},{10,2},{18,10},{26,18},{... | collective-permute-start | bytes 12296 | tf_op jit(solution)/shard_map/ppermute | solution.py:14
  11.3 0.7 copy-start.9
  13.7 17.6 %all-to-all-start = ((f32[1,4,16]{2,0,1:T(1,128)}), f32[1,4,16]{2,0,1:T(1,128)S(1)}, u32[]{:S(2)}, u32[]{:S(2)}) async-start(f32[1,4,16]{2,0,1:T(1,128)} %bitcast.23), calls=%async_computation | async-start | bytes 4096 | tf_op jit(solution)/shard_map/all_to_all | solution.py:149
  18.7 1.0 copy-start.7
  19.6 7.9 %copy-start = (f32[1,9,8,8,128]{4,3,2,1,0:T(8,128)S(1)}, f32[1,9,8,8,128]{4,3,2,1,0:T(8,128)}, u32[]{:S(2)}) copy-start(f32[1,9,8,8,128]{4,3,2,1,0:T(8,128)} %param.63) | copy-start | bytes 884740
  19.7 5.2 %copy-start.6 = (s32[2]{0:T(128)S(1)}, s32[2]{0:T(128)}, u32[]{:S(2)}) copy-start(s32[2]{0:T(128)} %constant.871) | copy-start | bytes 28
  19.7 8.6 %copy-start.11 = (s32[2]{0:T(128)S(1)}, s32[2]{0:T(128)}, u32[]{:S(2)}) copy-start(s32[2]{0:T(128)} %constant.872) | copy-start | bytes 28
  19.7 8.6 %copy-start.10 = (s32[2]{0:T(128)S(1)}, s32[2]{0:T(128)}, u32[]{:S(2)}) copy-start(s32[2]{0:T(128)} %constant.881) | copy-start | bytes 28
  19.7 8.6 %copy-start.5 = (s32[2]{0:T(128)S(1)}, s32[2]{0:T(128)}, u32[]{:S(2)}) copy-start(s32[2]{0:T(128)} %constant.884) | copy-start | bytes 28
  19.7 8.6 %copy-start.8 = (f32[1,32,9]{1,0,2:T(1,128)S(1)}, f32[1,32,9]{1,0,2:T(1,128)}, u32[]{:S(2)}) copy-start(f32[1,32,9]{1,0,2:T(1,128)} %param.70) | copy-start | bytes 3460
  19.7 9.4 %copy-start.4 = (f32[8,8,128]{2,1,0:T(8,128)S(1)}, f32[8,8,128]{2,1,0:T(8,128)}, u32[]{:S(2)}) copy-start(f32[8,8,128]{2,1,0:T(8,128)} %param.65) | copy-start | bytes 98308
  20.3 15.6 %collective-permute-start.2 = (f32[1,2,1,8,128]{4,3,1,2,0:T(8,128)S(1)}, f32[1,2,1,8,128]{4,3,1,2,0:T(8,128)S(1)}, u32[]{:S(2)}, u32[]{:S(2)}) collective-permute-start(f32[1,2,1,8,128]{4,3,1,2,0:T(8,128)S(1)} %bitcast.607), channel_id=1, source_target_pairs={{0,8},{8,16},{16,24},{1,9},{9,17},{17,25},{2,10},{10,18},{18,26},{... | collective-permute-start | bytes 24584 | tf_op jit(solution)/shard_map/ppermute | solution.py:14
  24.7 5.1 %copy-start.1 = (bf16[1,3,9,8,8,128]{5,4,3,2,1,0:T(8,128)(2,1)S(1)}, bf16[1,3,9,8,8,128]{5,4,3,2,1,0:T(8,128)(2,1)}, u32[]{:S(2)}) copy-start(bf16[1,3,9,8,8,128]{5,4,3,2,1,0:T(8,128)(2,1)} %param.64) | copy-start | bytes 1327108
  25.4 10.6 %collective-permute-start.1 = (f32[1,2,8,1,128]{4,2,3,1,0:T(8,128)S(1)}, f32[1,2,8,1,128]{4,2,3,1,0:T(8,128)S(1)}, u32[]{:S(2)}, u32[]{:S(2)}) collective-permute-start(f32[1,2,8,1,128]{4,2,3,1,0:T(8,128)S(1)} %bitcast.606), channel_id=1, source_target_pairs={{0,2},{2,4},{4,6},{1,3},{3,5},{5,7},{8,10},{10,12},{12,14},{9,11},... | collective-permute-start | bytes 24584 | tf_op jit(solution)/shard_map/ppermute | solution.py:14
  29.1 0.8 copy-start.3
  31.3 7.2 %all-to-all-start.1 = ((f32[1,64,3]{2,0,1:T(1,128)}), f32[1,64,3]{2,0,1:T(1,128)S(1)}, u32[]{:S(2)}, u32[]{:S(2)}) async-start(f32[1,64,3]{2,0,1:T(1,128)} %bitcast.28), calls=%async_computation.1 | async-start | bytes 65536 | tf_op jit(solution)/shard_map/all_to_all | solution.py:142
  38.5 33.0 %all-to-all-start.2 = ((f32[1,64,3]{2,0,1:T(1,128)}), f32[1,64,3]{2,0,1:T(1,128)S(1)}, u32[]{:S(2)}, u32[]{:S(2)}) async-start(f32[1,64,3]{2,0,1:T(1,128)} %bitcast.72), calls=%async_computation.2 | async-start | bytes 65536 | tf_op jit(solution)/shard_map/all_to_all | solution.py:142
  43.2 10.0 %collective-permute-start.4 = (f32[1,1,1,8,128]{4,3,2,1,0:T(8,128)S(1)}, f32[1,1,1,8,128]{4,3,2,1,0:T(8,128)S(1)}, u32[]{:S(2)}, u32[]{:S(2)}) collective-permute-start(f32[1,1,1,8,128]{4,3,2,1,0:T(8,128)S(1)} %slice.1093), channel_id=1, source_target_pairs={{0,8},{8,16},{16,24},{1,9},{9,17},{17,25},{2,10},{10,18},{18,26},{... | collective-permute-start | bytes 12296 | tf_op jit(solution)/shard_map/ppermute | solution.py:14
  46.8 6.5 %collective-permute-start.5 = (f32[1,1,8,1,128]{4,3,2,1,0:T(1,128)S(1)}, f32[1,1,8,1,128]{4,3,2,1,0:T(1,128)S(1)}, u32[]{:S(2)}, u32[]{:S(2)}) collective-permute-start(f32[1,1,8,1,128]{4,3,2,1,0:T(1,128)S(1)} %slice.1096), channel_id=1, source_target_pairs={{0,2},{2,4},{4,6},{1,3},{3,5},{5,7},{8,10},{10,12},{12,14},{9,11},... | collective-permute-start | bytes 12296 | tf_op jit(solution)/shard_map/ppermute | solution.py:14
  48.9 5.5 %collective-permute-start.7 = (f32[1,2,1,8,128]{4,3,1,2,0:T(8,128)S(1)}, f32[1,2,1,8,128]{4,3,1,2,0:T(8,128)S(1)}, u32[]{:S(2)}, u32[]{:S(2)}) collective-permute-start(f32[1,2,1,8,128]{4,3,1,2,0:T(8,128)S(1)} %bitcast.613), channel_id=1, source_target_pairs={{8,0},{16,8},{24,16},{9,1},{17,9},{25,17},{10,2},{18,10},{26,18},{... | collective-permute-start | bytes 24584 | tf_op jit(solution)/shard_map/ppermute | solution.py:14
  50.7 4.5 %collective-permute-start.6 = (f32[1,2,8,1,128]{4,2,3,1,0:T(8,128)S(1)}, f32[1,2,8,1,128]{4,2,3,1,0:T(8,128)S(1)}, u32[]{:S(2)}, u32[]{:S(2)}) collective-permute-start(f32[1,2,8,1,128]{4,2,3,1,0:T(8,128)S(1)} %bitcast.617), channel_id=1, source_target_pairs={{2,0},{4,2},{6,4},{3,1},{5,3},{7,5},{10,8},{12,10},{14,12},{11,9},... | collective-permute-start | bytes 24584 | tf_op jit(solution)/shard_map/ppermute | solution.py:14
  55.4 0.8 copy-start.2
  56.4 14.0 %collective-permute-start.11 = (f32[1,1,8,1,128]{4,3,2,1,0:T(1,128)S(1)}, f32[1,1,8,1,128]{4,3,2,1,0:T(1,128)S(1)}, u32[]{:S(2)}, u32[]{:S(2)}) collective-permute-start(f32[1,1,8,1,128]{4,3,2,1,0:T(1,128)S(1)} %slice.1121), channel_id=1, source_target_pairs={{2,0},{4,2},{6,4},{3,1},{5,3},{7,5},{10,8},{12,10},{14,12},{11,9},... | collective-permute-start | bytes 12296 | tf_op jit(solution)/shard_map/ppermute | solution.py:14
  58.2 12.1 %collective-permute-start.10 = (f32[1,2,1,8,128]{4,3,1,2,0:T(8,128)S(1)}, f32[1,2,1,8,128]{4,3,1,2,0:T(8,128)S(1)}, u32[]{:S(2)}, u32[]{:S(2)}) collective-permute-start(f32[1,2,1,8,128]{4,3,1,2,0:T(8,128)S(1)} %bitcast.614), channel_id=1, source_target_pairs={{0,8},{8,16},{16,24},{1,9},{9,17},{17,25},{2,10},{10,18},{18,26},{... | collective-permute-start | bytes 24584 | tf_op jit(solution)/shard_map/ppermute | solution.py:14
  64.3 6.2 %collective-permute-start.8 = (f32[1,1,1,8,128]{4,3,2,1,0:T(8,128)S(1)}, f32[1,1,1,8,128]{4,3,2,1,0:T(8,128)S(1)}, u32[]{:S(2)}, u32[]{:S(2)}) collective-permute-start(f32[1,1,1,8,128]{4,3,2,1,0:T(8,128)S(1)} %slice.1101), channel_id=1, source_target_pairs={{8,0},{16,8},{24,16},{9,1},{17,9},{25,17},{10,2},{18,10},{26,18},{... | collective-permute-start | bytes 12296 | tf_op jit(solution)/shard_map/ppermute | solution.py:14
  65.7 5.5 %collective-permute-start.9 = (f32[1,2,8,1,128]{4,2,3,1,0:T(8,128)S(1)}, f32[1,2,8,1,128]{4,2,3,1,0:T(8,128)S(1)}, u32[]{:S(2)}, u32[]{:S(2)}) collective-permute-start(f32[1,2,8,1,128]{4,2,3,1,0:T(8,128)S(1)} %bitcast.615), channel_id=1, source_target_pairs={{0,2},{2,4},{4,6},{1,3},{3,5},{5,7},{8,10},{10,12},{12,14},{9,11},... | collective-permute-start | bytes 24584 | tf_op jit(solution)/shard_map/ppermute | solution.py:14
  72.9 17.8 %collective-permute-start.15 = (f32[1,2,1,8,128]{4,3,1,2,0:T(8,128)S(1)}, f32[1,2,1,8,128]{4,3,1,2,0:T(8,128)S(1)}, u32[]{:S(2)}, u32[]{:S(2)}) collective-permute-start(f32[1,2,1,8,128]{4,3,1,2,0:T(8,128)S(1)} %bitcast.608), channel_id=1, source_target_pairs={{8,0},{16,8},{24,16},{9,1},{17,9},{25,17},{10,2},{18,10},{26,18},{... | collective-permute-start | bytes 24584 | tf_op jit(solution)/shard_map/ppermute | solution.py:14
  74.7 15.9 %collective-permute-start.14 = (f32[1,2,8,1,128]{4,2,3,1,0:T(8,128)S(1)}, f32[1,2,8,1,128]{4,2,3,1,0:T(8,128)S(1)}, u32[]{:S(2)}, u32[]{:S(2)}) collective-permute-start(f32[1,2,8,1,128]{4,2,3,1,0:T(8,128)S(1)} %bitcast.610), channel_id=1, source_target_pairs={{2,0},{4,2},{6,4},{3,1},{5,3},{7,5},{10,8},{12,10},{14,12},{11,9},... | collective-permute-start | bytes 24584 | tf_op jit(solution)/shard_map/ppermute | solution.py:14
  76.1 14.5 %collective-permute-start.12 = (f32[1,1,1,8,128]{4,3,2,1,0:T(8,128)S(1)}, f32[1,1,1,8,128]{4,3,2,1,0:T(8,128)S(1)}, u32[]{:S(2)}, u32[]{:S(2)}) collective-permute-start(f32[1,1,1,8,128]{4,3,2,1,0:T(8,128)S(1)} %slice.1130), channel_id=1, source_target_pairs={{0,8},{8,16},{16,24},{1,9},{9,17},{17,25},{2,10},{10,18},{18,26},{... | collective-permute-start | bytes 12296 | tf_op jit(solution)/shard_map/ppermute | solution.py:14
  81.0 9.7 %collective-permute-start.13 = (f32[1,1,8,1,128]{4,3,2,1,0:T(1,128)S(1)}, f32[1,1,8,1,128]{4,3,2,1,0:T(1,128)S(1)}, u32[]{:S(2)}, u32[]{:S(2)}) collective-permute-start(f32[1,1,8,1,128]{4,3,2,1,0:T(1,128)S(1)} %slice.1133), channel_id=1, source_target_pairs={{0,2},{2,4},{4,6},{1,3},{3,5},{5,7},{8,10},{10,12},{12,14},{9,11},... | collective-permute-start | bytes 12296 | tf_op jit(solution)/shard_map/ppermute | solution.py:14
  85.5 19.9 %all-to-all-start.3 = ((f32[1,64,3]{2,0,1:T(1,128)}), f32[1,64,3]{2,0,1:T(1,128)S(1)}, u32[]{:S(2)}, u32[]{:S(2)}) async-start(f32[1,64,3]{2,0,1:T(1,128)} %bitcast.116), calls=%async_computation.3 | async-start | bytes 65536 | tf_op jit(solution)/shard_map/all_to_all | solution.py:142
  89.4 58.1 %all-reduce.33.cloned.1.call-start = ((), (), s32[]{:S(2)}) async-start(), calls=%async_computation.4 | async-start | bytes 196608 | tf_op jit(solution)/shard_map/psum | solution.py:168
  91.1 13.2 %collective-permute-start.19 = (f32[1,1,8,1,128]{4,3,2,1,0:T(1,128)S(1)}, f32[1,1,8,1,128]{4,3,2,1,0:T(1,128)S(1)}, u32[]{:S(2)}, u32[]{:S(2)}) collective-permute-start(f32[1,1,8,1,128]{4,3,2,1,0:T(1,128)S(1)} %slice.1158), channel_id=1, source_target_pairs={{2,0},{4,2},{6,4},{3,1},{5,3},{7,5},{10,8},{12,10},{14,12},{11,9},... | collective-permute-start | bytes 12296 | tf_op jit(solution)/shard_map/ppermute | solution.py:14
  93.0 11.3 %collective-permute-start.18 = (f32[1,2,1,8,128]{4,3,1,2,0:T(8,128)S(1)}, f32[1,2,1,8,128]{4,3,1,2,0:T(8,128)S(1)}, u32[]{:S(2)}, u32[]{:S(2)}) collective-permute-start(f32[1,2,1,8,128]{4,3,1,2,0:T(8,128)S(1)} %bitcast.611), channel_id=1, source_target_pairs={{0,8},{8,16},{16,24},{1,9},{9,17},{17,25},{2,10},{10,18},{18,26},{... | collective-permute-start | bytes 24584 | tf_op jit(solution)/shard_map/ppermute | solution.py:14
  98.7 5.7 %collective-permute-start.16 = (f32[1,1,1,8,128]{4,3,2,1,0:T(8,128)S(1)}, f32[1,1,1,8,128]{4,3,2,1,0:T(8,128)S(1)}, u32[]{:S(2)}, u32[]{:S(2)}) collective-permute-start(f32[1,1,1,8,128]{4,3,2,1,0:T(8,128)S(1)} %slice.1138), channel_id=1, source_target_pairs={{8,0},{16,8},{24,16},{9,1},{17,9},{25,17},{10,2},{18,10},{26,18},{... | collective-permute-start | bytes 12296 | tf_op jit(solution)/shard_map/ppermute | solution.py:14
  100.1 5.0 %collective-permute-start.17 = (f32[1,2,8,1,128]{4,2,3,1,0:T(8,128)S(1)}, f32[1,2,8,1,128]{4,2,3,1,0:T(8,128)S(1)}, u32[]{:S(2)}, u32[]{:S(2)}) collective-permute-start(f32[1,2,8,1,128]{4,2,3,1,0:T(8,128)S(1)} %bitcast.612), channel_id=1, source_target_pairs={{0,2},{2,4},{4,6},{1,3},{3,5},{5,7},{8,10},{10,12},{12,14},{9,11},... | collective-permute-start | bytes 24584 | tf_op jit(solution)/shard_map/ppermute | solution.py:14
  106.9 13.1 %collective-permute-start.20 = (f32[1,1,1,8,128]{4,3,2,1,0:T(8,128)S(1)}, f32[1,1,1,8,128]{4,3,2,1,0:T(8,128)S(1)}, u32[]{:S(2)}, u32[]{:S(2)}) collective-permute-start(f32[1,1,1,8,128]{4,3,2,1,0:T(8,128)S(1)} %slice.1167), channel_id=1, source_target_pairs={{0,8},{8,16},{16,24},{1,9},{9,17},{17,25},{2,10},{10,18},{18,26},{... | collective-permute-start | bytes 12296 | tf_op jit(solution)/shard_map/ppermute | solution.py:14
  111.2 8.8 %collective-permute-start.21 = (f32[1,1,8,1,128]{4,3,2,1,0:T(1,128)S(1)}, f32[1,1,8,1,128]{4,3,2,1,0:T(1,128)S(1)}, u32[]{:S(2)}, u32[]{:S(2)}) collective-permute-start(f32[1,1,8,1,128]{4,3,2,1,0:T(1,128)S(1)} %slice.1170), channel_id=1, source_target_pairs={{0,2},{2,4},{4,6},{1,3},{3,5},{5,7},{8,10},{10,12},{12,14},{9,11},... | collective-permute-start | bytes 12296 | tf_op jit(solution)/shard_map/ppermute | solution.py:14
  115.1 5.5 %collective-permute-start.23 = (f32[1,2,1,8,128]{4,3,1,2,0:T(8,128)S(1)}, f32[1,2,1,8,128]{4,3,1,2,0:T(8,128)S(1)}, u32[]{:S(2)}, u32[]{:S(2)}) collective-permute-start(f32[1,2,1,8,128]{4,3,1,2,0:T(8,128)S(1)} %bitcast.609), channel_id=1, source_target_pairs={{8,0},{16,8},{24,16},{9,1},{17,9},{25,17},{10,2},{18,10},{26,18},{... | collective-permute-start | bytes 24584 | tf_op jit(solution)/shard_map/ppermute | solution.py:14
  116.9 5.1 %collective-permute-start.22 = (f32[1,2,8,1,128]{4,2,3,1,0:T(8,128)S(1)}, f32[1,2,8,1,128]{4,2,3,1,0:T(8,128)S(1)}, u32[]{:S(2)}, u32[]{:S(2)}) collective-permute-start(f32[1,2,8,1,128]{4,2,3,1,0:T(8,128)S(1)} %bitcast.616), channel_id=1, source_target_pairs={{2,0},{4,2},{6,4},{3,1},{5,3},{7,5},{10,8},{12,10},{14,12},{11,9},... | collective-permute-start | bytes 24584 | tf_op jit(solution)/shard_map/ppermute | solution.py:14
Sparse Core Ops, SparseCore 0:
  123.9 23.6 all-reduce.32
where the time goes:
time: 157 us; the launch traced here: 156 us
  starting transfers between devices  77.9 us (50%)
  waiting for transfers between devices  30.6 us (19%)
  local copies, waits for them, and re-layouts  23.6 us (15%)
  between operations  15.9 us (10%)
  other arithmetic  6.52 us (4%)
    ppermute x24, starting transfers between devices, passed_along(): lax.ppermute(value, axis, [(source, source + steps) for source in range(l...  62.4 us
    psum x1, waiting for transfers between devices, on_device(): lax.psum((jnp.sum(rho_kernel, axis=0), jnp.sum(lambda_kernel, axis=0), jn...  23.1 us
    all_to_all x3, starting transfers between devices, on_device(): lax.all_to_all(send_values[:, :, 3 * step:3 * step + 3], 'sy', split_axis...  10.5 us
    ppermute x24, waiting for transfers between devices, passed_along(): lax.ppermute(value, axis, [(source, source + steps) for source in range(l...  5.36 us
    all_to_all x1, starting transfers between devices, on_device(): lax.all_to_all(send_cells, 'sy', split_axis=1, concat_axis=1, tiled=True)  4.96 us
  transfers between devices with their start and end apart: 29, of which 8 were waited for; matrix products, arithmetic and copies ran while one was open for 15% of the time, Pallas kernels for 0%

commit v1 on v0

v1 whole, which is shorter than its diff:
```python
import functools

import jax
import jax.numpy as jnp
from jax import lax
from jax.experimental import pallas as pl
from jax.experimental.pallas import tpu as pltpu
from jax.sharding import PartitionSpec as P

DT = 0.35
MESH = pl.DeviceIdType.MESH

STRESS_FACES = ((3,), (6, 7), (4,), (6, 8))
VELOCITY_FACES = ((1, 2), (0,), (0, 2), (1,))


def kernel(
    n_sx, n_sy, n_ev, cx, cy, cz, steps, owned,
    adj, fwd, inv_density, lame, shear, blocks, cells, traces, counts,
    state, total,
    fwd_v, dens_v, lame_v, shear_v, blocks_v, cells_v, traces_v, counts_v,
    plane_out, plane_in, rows_out, rows_in, kern_in,
    load_sem, face_send, face_recv, rows_send, rows_recv, kern_send, kern_recv,
):
    ix, iy, ie = lax.axis_index("sx"), lax.axis_index("sy"), lax.axis_index("ev")
    area = cx * cy

    pairs = [
        (traces, traces_v), (blocks, blocks_v), (counts, counts_v), (cells, cells_v),
        (adj, state), (inv_density, dens_v), (fwd, fwd_v), (lame, lame_v), (shear, shear_v),
    ]
    loads = [pltpu.make_async_copy(a, b, load_sem.at[i]) for i, (a, b) in enumerate(pairs)]
    for load in loads:
        load.start()

    goes = (ix > 0, ix < n_sx - 1, iy > 0, iy < n_sy - 1)
    comes = (ix < n_sx - 1, ix > 0, iy < n_sy - 1, iy > 0)
    targets = ({"sx": ix - 1}, {"sx": ix + 1}, {"sy": iy - 1}, {"sy": iy + 1})

    barrier = pltpu.get_barrier_semaphore()
    for side in (0, 1):
        @pl.when(goes[side])
        def _(side=side):
            pl.semaphore_signal(barrier, inc=1, device_id=targets[side], device_id_type=MESH)
    for d in range(1, n_sy):
        pl.semaphore_signal(barrier, inc=1, device_id={"sy": lax.rem(iy + d, n_sy)}, device_id_type=MESH)
    for d in range(1, n_ev):
        pl.semaphore_signal(barrier, inc=1, device_id={"ev": lax.rem(ie + d, n_ev)}, device_id_type=MESH)

    for side in range(4):
        @pl.when(jnp.logical_not(comes[side]))
        def _(side=side):
            plane_in[:, side] = jnp.zeros((2 * steps, 2, max(cx, cy), cz), jnp.float32)

    for load in loads[:4]:
        load.wait()
    row = lax.broadcasted_iota(jnp.int32, (owned, 1), 0)
    live = row < counts_v[...]
    lanes_used = traces_v.shape[1]
    for d in range(n_sy):
        goal = lax.rem(iy + d, n_sy)
        keep = jnp.logical_and(live, blocks_v[...] == goal)
        rows_out[d, :owned, :] = jnp.zeros((owned, 128), jnp.float32)
        rows_out[d, :owned, :lanes_used] = jnp.where(keep, traces_v[...], 0.0)
        rows_out[d, owned:, :] = jnp.zeros((8, 128), jnp.float32)
        rows_out[d, owned:owned + 1, :owned] = cells_v[...].astype(jnp.float32)

    amount = (n_sy - 1) + (n_ev - 1) + (ix > 0).astype(jnp.int32) + (ix < n_sx - 1).astype(jnp.int32)
    pl.semaphore_wait(barrier, amount)

    def face_copy(turn, side, count):
        return pltpu.make_async_remote_copy(
            src_ref=plane_out.at[turn, side, pl.ds(0, count)],
            dst_ref=plane_in.at[turn, side, pl.ds(0, count)],
            send_sem=face_send.at[turn, side],
            recv_sem=face_recv.at[turn, side],
            device_id=targets[side],
            device_id_type=MESH,
        )

    def send_faces(turn, faces):
        for side, fields in enumerate(faces):
            for i, f in enumerate(fields):
                if side == 0:
                    plane_out[turn, side, i, :cy] = state[f, 0:cy, :]
                elif side == 1:
                    plane_out[turn, side, i, :cy] = state[f, area - cy:area, :]
                else:
                    at = 0 if side == 2 else cy - 1
                    plane_out[turn, side, i, :cx] = state[f, pl.ds(at, cx, stride=cy), :]

            @pl.when(goes[side])
            def _(side=side, fields=fields):
                face_copy(turn, side, len(fields)).start()

    def receive_faces(turn, faces):
        for side, fields in enumerate(faces):
            @pl.when(comes[side])
            def _(side=side, fields=fields):
                face_copy(turn, side, len(fields)).wait_recv()

    def rows_copy(d):
        return pltpu.make_async_remote_copy(
            src_ref=rows_out.at[d],
            dst_ref=rows_in.at[d - 1],
            send_sem=rows_send.at[d - 1],
            recv_sem=rows_recv.at[d - 1],
            device_id={"sy": lax.rem(iy + d, n_sy)},
            device_id_type=MESH,
        )

    def kern_copy(d, first, count, part):
        return pltpu.make_async_remote_copy(
            src_ref=total.at[pl.ds(first, count)],
            dst_ref=kern_in.at[d - 1, pl.ds(first, count)],
            send_sem=kern_send.at[d - 1, part],
            recv_sem=kern_recv.at[d - 1, part],
            device_id={"ev": lax.rem(ie + d, n_ev)},
            device_id_type=MESH,
        )

    loads[4].wait()
    send_faces(0, STRESS_FACES)
    for d in range(1, n_sy):
        rows_copy(d).start()
    for load in loads[5:]:
        load.wait()

    lane = lax.broadcasted_iota(jnp.int32, (area, cz), 1)
    y_at = lax.rem(lax.broadcasted_iota(jnp.int32, (area, cz), 0), cy)
    first_z, last_z = lane == 0, lane == cz - 1
    first_y, last_y = y_at == 0, y_at == cy - 1

    def above(f):
        return jnp.where(last_z, 0.0, pltpu.roll(f, cz - 1, 1))

    def below(f):
        return jnp.where(first_z, 0.0, pltpu.roll(f, 1, 1))

    def next_x(f, turn, i):
        return jnp.concatenate([f[cy:], plane_in[turn, 0, i, :cy]], axis=0)

    def prev_x(f, turn, i):
        return jnp.concatenate([plane_in[turn, 1, i, :cy], f[:area - cy]], axis=0)

    def spread(turn, side, i):
        return jnp.concatenate(
            [jnp.broadcast_to(plane_in[turn, side, i, x:x + 1], (cy, cz)) for x in range(cx)], axis=0
        )

    def next_y(f, turn, i):
        return jnp.where(last_y, spread(turn, 2, i), pltpu.roll(f, area - 1, 0))

    def prev_y(f, turn, i):
        return jnp.where(first_y, spread(turn, 3, i), pltpu.roll(f, 1, 0))

    def forward(step, f):
        return fwd_v[step, f].astype(jnp.float32).reshape(area, cz)

    def scattered(rows):
        cell = lax.broadcasted_iota(jnp.int32, (area, owned), 0).astype(jnp.float32)
        table = (cell == rows[owned:owned + 1, :owned]).astype(jnp.float32)
        return jnp.dot(
            table, rows[:owned, :], precision=lax.Precision.HIGHEST, preferred_element_type=jnp.float32
        )

    surface = scattered(rows_out.at[0])
    for d in range(1, n_sy):
        rows_copy(d).wait_recv()
        surface = surface + scattered(rows_in.at[d - 1])

    def force(k):
        moved = surface if k == 0 else pltpu.roll(surface, 128 - k, 1)
        return jnp.where(first_z, moved, 0.0)

    for step in range(steps):
        last = step == steps - 1
        turn = 2 * step
        forces = [force(3 * step + c) for c in range(3)]
        receive_faces(turn, STRESS_FACES)
        sxx, syy, szz, sxy, sxz, syz = [state[3 + c] for c in range(6)]
        accel_x = (next_x(sxx, turn, 0) - sxx) + (sxy - prev_y(sxy, turn, 0)) + (sxz - below(sxz))
        accel_y = (sxy - prev_x(sxy, turn, 0)) + (next_y(syy, turn, 0) - syy) + (syz - below(syz))
        accel_z = (sxz - prev_x(sxz, turn, 1)) + (syz - prev_y(syz, turn, 1)) + (above(szz) - szz)
        scale = DT * dens_v[...]
        change = [scale * (a + f) for a, f in zip((accel_x, accel_y, accel_z), forces)]
        for c in range(3):
            state[c] = state[c] + change[c]
        turn += 1
        send_faces(turn, VELOCITY_FACES)

        rho = sum(forward(step, c) * change[c] for c in range(3))
        total[0] = rho if step == 0 else total[0] + rho
        if last:
            for d in range(1, n_ev):
                kern_copy(d, 0, 1, 0).start()
        strain = [forward(step, 3 + c) for c in range(6)]

        receive_faces(turn, VELOCITY_FACES)
        vx, vy, vz = [state[c] for c in range(3)]
        exx = vx - prev_x(vx, turn, 0)
        eyy = vy - prev_y(vy, turn, 0)
        ezz = vz - below(vz)
        exy = 0.5 * ((next_y(vx, turn, 0) - vx) + (next_x(vy, turn, 0) - vy))
        exz = 0.5 * ((above(vx) - vx) + (next_x(vz, turn, 1) - vz))
        eyz = 0.5 * ((above(vy) - vy) + (next_y(vz, turn, 1) - vz))
        rates = (exx, eyy, ezz, exy, exz, eyz)
        trace = exx + eyy + ezz

        def update_stress():
            mu = (DT * 2.0) * shear_v[...]
            common = DT * lame_v[...] * trace
            for c in range(6):
                moved = mu * rates[c]
                state[3 + c] = state[3 + c] + (moved + common if c < 3 else moved)

        def update_kernels():
            lam = DT * (strain[0] + strain[1] + strain[2]) * trace
            diagonal = strain[0] * exx + strain[1] * eyy + strain[2] * ezz
            others = strain[3] * exy + strain[4] * exz + strain[5] * eyz
            she = (DT * 2.0) * (diagonal + 2.0 * others)
            total[1] = lam if step == 0 else total[1] + lam
            total[2] = she if step == 0 else total[2] + she

        if last:
            update_kernels()
            for d in range(1, n_ev):
                kern_copy(d, 1, 2, 1).start()
            update_stress()
        else:
            update_stress()
            send_faces(turn + 1, STRESS_FACES)
            update_kernels()

    for step in range(steps):
        for turn, faces in ((2 * step, STRESS_FACES), (2 * step + 1, VELOCITY_FACES)):
            for side, fields in enumerate(faces):
                @pl.when(goes[side])
                def _(turn=turn, side=side, fields=fields):
                    face_copy(turn, side, len(fields)).wait_send()
    for d in range(1, n_sy):
        rows_copy(d).wait_send()
    for d in range(1, n_ev):
        kern_copy(d, 0, 1, 0).wait()
        kern_copy(d, 1, 2, 1).wait()
    for c in range(3):
        value = total[c]
        for d in range(1, n_ev):
            value = value + kern_in[d - 1, c]
        total[c] = value


def on_device(
    sizes,
    adjoint_state,
    forward_state,
    inv_density,
    lame_lambda,
    shear_modulus,
    station_block,
    station_cell,
    station_trace,
    source_count,
):
    n_sx, n_sy, n_ev = sizes
    fields, cx, cy, cz = adjoint_state.shape[1:]
    steps = forward_state.shape[1]
    owned = station_cell.shape[1]
    area, wide = cx * cy, max(cx, cy)
    anywhere = pl.BlockSpec(memory_space=pl.ANY)
    vmem = pl.BlockSpec(memory_space=pltpu.VMEM)
    f32, i32 = jnp.float32, jnp.int32
    state, kernels = pl.pallas_call(
        functools.partial(kernel, n_sx, n_sy, n_ev, cx, cy, cz, steps, owned),
        out_shape=(
            jax.ShapeDtypeStruct((fields, area, cz), f32),
            jax.ShapeDtypeStruct((3, area, cz), f32),
        ),
        in_specs=[anywhere] * 9,
        out_specs=(vmem, vmem),
        scratch_shapes=[
            pltpu.VMEM((steps, fields, cx, cy, cz), jnp.bfloat16),
            pltpu.VMEM((area, cz), f32),
            pltpu.VMEM((area, cz), f32),
            pltpu.VMEM((area, cz), f32),
            pltpu.VMEM((owned, 1), i32),
            pltpu.VMEM((1, owned), i32),
            pltpu.VMEM((owned, 3 * steps), f32),
            pltpu.VMEM((1, 1), i32),
            pltpu.VMEM((2 * steps, 4, 2, wide, cz), f32),
            pltpu.VMEM((2 * steps, 4, 2, wide, cz), f32),
            pltpu.VMEM((n_sy, owned + 8, 128), f32),
            pltpu.VMEM((max(1, n_sy - 1), owned + 8, 128), f32),
            pltpu.VMEM((max(1, n_ev - 1), 3, area, cz), f32),
            pltpu.SemaphoreType.DMA((9,)),
            pltpu.SemaphoreType.DMA((2 * steps, 4)),
            pltpu.SemaphoreType.DMA((2 * steps, 4)),
            pltpu.SemaphoreType.DMA((max(1, n_sy - 1),)),
            pltpu.SemaphoreType.DMA((max(1, n_sy - 1),)),
            pltpu.SemaphoreType.DMA((max(1, n_ev - 1), 2)),
            pltpu.SemaphoreType.DMA((max(1, n_ev - 1), 2)),
        ],
        compiler_params=pltpu.CompilerParams(
            collective_id=0, has_side_effects=True, vmem_limit_bytes=24 * 1024 * 1024
        ),
    )(
        adjoint_state.reshape(fields, area, cz),
        forward_state[0],
        inv_density.reshape(area, cz),
        lame_lambda.reshape(area, cz),
        shear_modulus.reshape(area, cz),
        station_block[0],
        station_cell,
        station_trace[0],
        source_count,
    )
    return state.reshape(1, fields, cx, cy, cz), kernels.reshape(3, cx, cy, cz)


def solution(mesh):
    sizes = tuple(mesh.shape[name] for name in ("sx", "sy", "ev"))
    return jax.shard_map(
        functools.partial(on_device, sizes),
        mesh=mesh,
        in_specs=(
            P("ev", None, "sx", "sy", None),
            P("ev", None, None, "sx", "sy", None),
            P("sx", "sy", None),
            P("sx", "sy", None),
            P("sx", "sy", None),
            P("ev", ("sx", "sy"), None),
            P("ev", ("sx", "sy")),
            P("ev", ("sx", "sy"), None),
            P("ev", ("sx", "sy")),
        ),
        out_specs=(P("ev", None, "sx", "sy", None), P(None, "sx", "sy", None)),
        check_vma=False,
    )
```

time: 157 us -> 34.8 us (0.22)
  starting transfers between devices: 77.9 us -> 0 us
  waiting for transfers between devices: 30.6 us -> 0 us
  Pallas kernels: 0 us -> 26 us
  local copies, waits for them, and re-layouts: 23.6 us -> 7 us
  between operations: 15.9 us -> 1.31 us
  other arithmetic: 6.52 us -> 0 us
    ppermute x24 -> x0, starting transfers between devices: 62.4 us -> none  [passed_along(): lax.ppermute(value, axis, [(source, source + steps) for source in range(l...]
    pallas_call x0 -> x1, Pallas kernels: none -> 26 us  [on_device(): pl.pallas_call(functools.partial(kernel, n_sx, n_sy, n_ev, cx, cy, cz, st...]
    psum x1 -> x0, waiting for transfers between devices: 23.1 us -> none  [on_device(): lax.psum((jnp.sum(rho_kernel, axis=0), jnp.sum(lambda_kernel, axis=0), jn...]
    all_to_all x4 -> x0, starting transfers between devices: 15.4 us -> none  [the longest x3 10.5 us: on_device(): lax.all_to_all(send_values[:, :, 3 * step:3 * step + 3], 'sy', split_axis...]
    gather x36 -> x0, local copies, waits for them, and re-layouts: 14.8 us -> none  [the longest x6 2.43 us: border_planes(): high_y = passed_along(stack[:, faces[2], :, :1], 'sy', -1)]
    ppermute x24 -> x0, waiting for transfers between devices: 5.36 us -> none  [passed_along(): lax.ppermute(value, axis, [(source, source + steps) for source in range(l...]
    unnamed x30 -> x15, local copies, waits for them, and re-layouts: 2.22 us -> 6.27 us
    another operation x16 -> x0, other arithmetic: 3.52 us -> none  [the longest x3 2.68 us: on_device(): return (state, jnp.stack(totals, axis=0))]
  transfers between devices with their start and end apart: 29 -> 0, of which waited for: 8 -> 0; matrix products, arithmetic and copies ran while one was open for 15% -> 0% of each run, Pallas kernels for 0% -> 0%
where the time goes in v1:
time: 34.8 us; the launch traced here: 34.3 us
  Pallas kernels  26 us (75%)
  local copies, waits for them, and re-layouts  7 us (20%)
  between operations  1.31 us (4%)
    pallas_call x1, Pallas kernels, on_device(): pl.pallas_call(functools.partial(kernel, n_sx, n_sy, n_ev, cx, cy, cz, st...  26 us
    unnamed x15, local copies, waits for them, and re-layouts  6.27 us
    squeeze x1, local copies, waits for them, and re-layouts, on_device(): station_block[0]  0.74 us

profile of v1, /device:TPU:0, one launch (start us, length us, event | category | flops | bytes accessed | tf_op | source)
XLA Modules:
  0.0 34.3 jit_solution(6129045477753353863)
XLA Ops:
  0.6 0.0 copy-start.2
  1.3 0.7 %copy.12.blocks = s32[32,1]{1,0:T(8,128)S(1)} copy(s32[32,1]{0,1:T(1,128)} %bitcast.17) | data formatting | bytes 256 | tf_op jit(solution)/shard_map/squeeze | solution.py:312
  2.0 0.8 %copy.11 = f32[1,32,9]{2,1,0:T(8,128)S(1)} copy(f32[1,32,9]{1,0,2:T(1,128)} %param.16) | data formatting | bytes 2304 | tf_op args[7]
  2.8 0.0 copy-start.5
  2.8 0.0 copy-done.2
  2.8 0.7 %copy-done.5 = s32[1,32]{1,0:T(1,128)S(1)} copy-done((s32[1,32]{1,0:T(1,128)S(1)}, s32[1,32]{1,0:T(1,128)}, u32[]{:S(2)}) %copy-start.5) | copy-done | bytes 152
  3.5 0.0 copy-start
  3.5 1.0 %copy-done = bf16[1,3,9,8,8,128]{5,4,3,2,1,0:T(8,128)(2,1)S(1)} copy-done((bf16[1,3,9,8,8,128]{5,4,3,2,1,0:T(8,128)(2,1)S(1)}, bf16[1,3,9,8,8,128]{5,4,3,2,1,0:T(8,128)(2,1)}, u32[]{:S(2)}) %copy-start) | copy-done | bytes 442392
  4.5 0.0 copy-start.1
  4.5 1.0 %copy-done.1 = f32[1,9,8,8,128]{4,3,2,1,0:T(8,128)S(1)} copy-done((f32[1,9,8,8,128]{4,3,2,1,0:T(8,128)S(1)}, f32[1,9,8,8,128]{4,3,2,1,0:T(8,128)}, u32[]{:S(2)}) %copy-start.1) | copy-done | bytes 294936
  5.4 0.0 copy-start.3
  5.4 0.8 %copy-done.3 = f32[8,8,128]{2,1,0:T(8,128)S(1)} copy-done((f32[8,8,128]{2,1,0:T(8,128)S(1)}, f32[8,8,128]{2,1,0:T(8,128)}, u32[]{:S(2)}) %copy-start.3) | copy-done | bytes 32792
  6.2 0.0 copy-start.4
  6.2 0.8 %copy-done.4 = f32[8,8,128]{2,1,0:T(8,128)S(1)} copy-done((f32[8,8,128]{2,1,0:T(8,128)S(1)}, f32[8,8,128]{2,1,0:T(8,128)}, u32[]{:S(2)}) %copy-start.4) | copy-done | bytes 32792
  6.9 26.0 %shard_map.104 = (f32[9,64,128]{2,1,0:T(8,128)S(1)}, f32[3,64,128]{2,1,0:T(8,128)S(1)}) custom-call(f32[9,64,128]{2,1,0:T(8,128)S(1)} %bitcast.11, bf16[3,9,8,8,128]{4,3,2,1,0:T(8,128)(2,1)S(1)} %bitcast.9, f32[64,128]{1,0:T(8,128)S(1)} %bitcast.14, f32[64,128]{1,0:T(8,128)S(1)} %bitcast.15, f32[64,128]{1,0:T(8,128)S(1)} %bitcast.16, ...), custom_call_target="tpu_custom_call" | custom-call | tf_op jit(solution)/shard_map/pallas_call | solution.py:273
  33.0 0.7 %copy.16 = f32[1,9,8,8,128]{4,3,2,1,0:T(8,128)} copy(f32[1,9,8,8,128]{4,3,2,1,0:T(8,128)S(1)} %bitcast.10) | data formatting | bytes 589824
  33.7 0.6 %copy.17 = f32[3,8,8,128]{3,2,1,0:T(8,128)} copy(f32[3,8,8,128]{3,2,1,0:T(8,128)S(1)} %bitcast.12) | data formatting | bytes 196608
Async XLA Ops:
  0.6 2.2 %copy-start.2 = (f32[8,8,128]{2,1,0:T(8,128)S(1)}, f32[8,8,128]{2,1,0:T(8,128)}, u32[]{:S(2)}) copy-start(f32[8,8,128]{2,1,0:T(8,128)} %param.11) | copy-start | bytes 98308
  2.8 0.7 %copy-start.5 = (s32[1,32]{1,0:T(1,128)S(1)}, s32[1,32]{1,0:T(1,128)}, u32[]{:S(2)}) copy-start(s32[1,32]{1,0:T(1,128)} %cells.1) | copy-start | bytes 388
  3.5 1.0 %copy-start = (bf16[1,3,9,8,8,128]{5,4,3,2,1,0:T(8,128)(2,1)S(1)}, bf16[1,3,9,8,8,128]{5,4,3,2,1,0:T(8,128)(2,1)}, u32[]{:S(2)}) copy-start(bf16[1,3,9,8,8,128]{5,4,3,2,1,0:T(8,128)(2,1)} %param.10) | copy-start | bytes 1327108
  4.5 1.0 %copy-start.1 = (f32[1,9,8,8,128]{4,3,2,1,0:T(8,128)S(1)}, f32[1,9,8,8,128]{4,3,2,1,0:T(8,128)}, u32[]{:S(2)}) copy-start(f32[1,9,8,8,128]{4,3,2,1,0:T(8,128)} %param.9) | copy-start | bytes 884740
  5.4 0.8 %copy-start.3 = (f32[8,8,128]{2,1,0:T(8,128)S(1)}, f32[8,8,128]{2,1,0:T(8,128)}, u32[]{:S(2)}) copy-start(f32[8,8,128]{2,1,0:T(8,128)} %param.12) | copy-start | bytes 98308
  6.2 0.8 %copy-start.4 = (f32[8,8,128]{2,1,0:T(8,128)S(1)}, f32[8,8,128]{2,1,0:T(8,128)}, u32[]{:S(2)}) copy-start(f32[8,8,128]{2,1,0:T(8,128)} %param.13) | copy-start | bytes 98308

commit v2 on v1

v2 whole, which is shorter than its diff:
```python
import functools

import jax
import jax.numpy as jnp
from jax import lax
from jax.experimental import pallas as pl
from jax.experimental.pallas import tpu as pltpu
from jax.sharding import PartitionSpec as P

DT = 0.35
MESH = pl.DeviceIdType.MESH

STRESS_FACES = ((3,), (6, 7), (4,), (6, 8))
VELOCITY_FACES = ((1, 2), (0,), (0, 2), (1,))


def kernel(
    n_sx, n_sy, n_ev, cx, cy, cz, steps, owned,
    adj, fwd, inv_density, lame, shear, blocks, cells, traces, counts,
    state_out, total_out,
    state, total, forces, fwd_v, dens_v, lame_v, shear_v, blocks_v, cells_v, traces_v,
    plane_out, plane_in, corner_out, corner_in, rows_out, rows_in, kern_in,
    load_sem, store_sem, face_send, face_recv, corner_send, corner_recv, rows_send, rows_recv, kern_send, kern_recv,
):
    ix, iy, ie = lax.axis_index("sx"), lax.axis_index("sy"), lax.axis_index("ev")
    area = cx * cy

    pairs = [
        (traces, traces_v), (blocks, blocks_v), (cells, cells_v),
        (inv_density, dens_v), (adj, state), (fwd, fwd_v), (lame, lame_v), (shear, shear_v),
    ]
    loads = [pltpu.make_async_copy(a, b, load_sem.at[i]) for i, (a, b) in enumerate(pairs)]
    for load in loads:
        load.start()

    goes = (ix > 0, ix < n_sx - 1, iy > 0, iy < n_sy - 1)
    comes = (ix < n_sx - 1, ix > 0, iy < n_sy - 1, iy > 0)
    targets = ({"sx": ix - 1}, {"sx": ix + 1}, {"sy": iy - 1}, {"sy": iy + 1})
    corners = ((0, 2), (0, 3), (1, 2), (1, 3))
    corner_goes = [jnp.logical_and(goes[a], goes[b]) for a, b in corners]
    corner_comes = [jnp.logical_and(comes[a], comes[b]) for a, b in corners]
    corner_targets = [{**targets[a], **targets[b]} for a, b in corners]
    turns = steps + 1

    barrier = pltpu.get_barrier_semaphore()
    for side in (0, 1):
        @pl.when(goes[side])
        def _(side=side):
            pl.semaphore_signal(barrier, inc=1, device_id=targets[side], device_id_type=MESH)
    for g in range(4):
        @pl.when(corner_goes[g])
        def _(g=g):
            pl.semaphore_signal(barrier, inc=1, device_id=corner_targets[g], device_id_type=MESH)
    for d in range(1, n_sy):
        pl.semaphore_signal(barrier, inc=1, device_id={"sy": lax.rem(iy + d, n_sy)}, device_id_type=MESH)
    for d in range(1, n_ev):
        pl.semaphore_signal(barrier, inc=1, device_id={"ev": lax.rem(ie + d, n_ev)}, device_id_type=MESH)

    for side in range(4):
        @pl.when(jnp.logical_not(comes[side]))
        def _(side=side):
            plane_in[:, side] = jnp.zeros((turns, 3, max(cx, cy), cz), jnp.float32)
    for g in range(4):
        @pl.when(jnp.logical_not(corner_comes[g]))
        def _(g=g):
            corner_in[:, g] = jnp.zeros((turns, 8, cz), jnp.float32)
    corner_out[...] = jnp.zeros(corner_out.shape, jnp.float32)

    for load in loads[:3]:
        load.wait()
    comps = 3 * steps
    live = lax.broadcasted_iota(jnp.int32, (1, owned), 1) < counts[0, 0]
    for d in range(n_sy):
        goal = lax.rem(iy + d, n_sy)
        keep = jnp.logical_and(live, blocks_v[0] == goal)
        for k in range(comps):
            rows_out[d, k:k + 1, :owned] = jnp.where(keep, traces_v[k], 0.0)
        rows_out[d, comps:comps + 1, :owned] = cells_v[...].astype(jnp.float32)

    amount = (n_sy - 1) + (n_ev - 1) + (ix > 0).astype(jnp.int32) + (ix < n_sx - 1).astype(jnp.int32)
    for g in range(4):
        amount = amount + corner_goes[g].astype(jnp.int32)
    pl.semaphore_wait(barrier, amount)

    def face_copy(turn, side, count):
        return pltpu.make_async_remote_copy(
            src_ref=plane_out.at[turn, side, pl.ds(0, count)],
            dst_ref=plane_in.at[turn, side, pl.ds(0, count)],
            send_sem=face_send.at[turn, side],
            recv_sem=face_recv.at[turn, side],
            device_id=targets[side],
            device_id_type=MESH,
        )

    def corner_copy(turn, g):
        return pltpu.make_async_remote_copy(
            src_ref=corner_out.at[turn, g],
            dst_ref=corner_in.at[turn, g],
            send_sem=corner_send.at[turn, g],
            recv_sem=corner_recv.at[turn, g],
            device_id=corner_targets[g],
            device_id_type=MESH,
        )

    def edge(ref, side):
        if side == 0:
            return ref[0:cy, :]
        if side == 1:
            return ref[area - cy:area, :]
        return ref[pl.ds(0 if side == 2 else cy - 1, cx, stride=cy), :]

    def send_faces(turn, planes):
        for side, values in enumerate(planes):
            for i, value in enumerate(values):
                plane_out[turn, side, i, :value.shape[0]] = value

            @pl.when(goes[side])
            def _(side=side, count=len(values)):
                face_copy(turn, side, count).start()

    def receive_faces(turn, counts):
        for side in range(4):
            @pl.when(comes[side])
            def _(side=side):
                face_copy(turn, side, counts[side]).wait_recv()

    def send_corners(turn):
        for g, at, fields in ((0, 0, (4, 3)), (1, cy - 1, (8,)), (2, area - cy, (7,)), (3, area - 1, (6,))):
            for i, f in enumerate(fields):
                corner_out[turn, g, i:i + 1] = state[f, at:at + 1, :]

            @pl.when(corner_goes[g])
            def _(g=g):
                corner_copy(turn, g).start()

    def receive_corners(turn):
        for g in range(4):
            @pl.when(corner_comes[g])
            def _(g=g):
                corner_copy(turn, g).wait_recv()

    def rows_copy(d):
        return pltpu.make_async_remote_copy(
            src_ref=rows_out.at[d],
            dst_ref=rows_in.at[d - 1],
            send_sem=rows_send.at[d - 1],
            recv_sem=rows_recv.at[d - 1],
            device_id={"sy": lax.rem(iy + d, n_sy)},
            device_id_type=MESH,
        )

    def store(first, count, part):
        fields = pl.ds(first, count)
        return pltpu.make_async_copy(state.at[fields], state_out.at[fields], store_sem.at[part])

    def kern_copy(d, first, count, part):
        return pltpu.make_async_remote_copy(
            src_ref=total.at[pl.ds(first, count)],
            dst_ref=kern_in.at[d - 1, pl.ds(first, count)],
            send_sem=kern_send.at[d - 1, part],
            recv_sem=kern_recv.at[d - 1, part],
            device_id={"ev": lax.rem(ie + d, n_ev)},
            device_id_type=MESH,
        )

    loads[3].wait()
    loads[4].wait()
    send_faces(
        0,
        [[edge(state.at[f], side) for f in STRESS_FACES[side]] + [DT * edge(dens_v, side)] for side in range(4)],
    )
    for d in range(1, n_sy):
        rows_copy(d).start()
    for load in loads[5:]:
        load.wait()

    lane = lax.broadcasted_iota(jnp.int32, (area, cz), 1)
    y_at = lax.rem(lax.broadcasted_iota(jnp.int32, (area, cz), 0), cy)
    first_z, last_z = lane == 0, lane == cz - 1
    first_y, last_y = y_at == 0, y_at == cy - 1

    def above(f):
        return jnp.where(last_z[:f.shape[0]], 0.0, pltpu.roll(f, cz - 1, 1))

    def below(f):
        return jnp.where(first_z[:f.shape[0]], 0.0, pltpu.roll(f, 1, 1))

    def next_x(f, plane):
        return jnp.concatenate([f[cy:], plane], axis=0)

    def prev_x(f, plane):
        return jnp.concatenate([plane, f[:area - cy]], axis=0)

    def spread(plane):
        return jnp.concatenate([jnp.broadcast_to(plane[x:x + 1], (cy, cz)) for x in range(cx)], axis=0)

    def next_y(f, plane):
        return jnp.where(last_y, spread(plane), pltpu.roll(f, area - 1, 0))

    def prev_y(f, plane):
        return jnp.where(first_y, spread(plane), pltpu.roll(f, 1, 0))

    def up(plane):
        size = plane.shape[0]
        at = lax.broadcasted_iota(jnp.int32, plane.shape, 0)
        return jnp.where(at == size - 1, 0.0, pltpu.roll(plane, size - 1, 0))

    def down(plane):
        at = lax.broadcasted_iota(jnp.int32, plane.shape, 0)
        return jnp.where(at == 0, 0.0, pltpu.roll(plane, 1, 0))

    def on_row(row, at, size):
        place = lax.broadcasted_iota(jnp.int32, (size, cz), 0)
        return jnp.where(place == at, jnp.broadcast_to(row, (size, cz)), 0.0)

    def received(turn, side, i):
        return plane_in[turn, side, i, :cy if side < 2 else cx]

    def advanced(step):
        planes = []
        for side in range(4):
            vx, vy, vz, sxx, syy, szz, sxy, sxz, syz = [edge(state.at[f], side) for f in range(9)]
            fx, fy, fz = [edge(forces.at[3 * step + c], side) for c in range(3)]
            scale = DT * edge(dens_v, side)
            if side == 0:
                y = vy + scale * (sxy + (up(syy) - syy) + (syz - below(syz)) + fy)
                z = vz + scale * (sxz + (syz - down(syz)) + (above(szz) - szz) + fz)
                planes.append([sxx, y, z])
            elif side == 1:
                x = vx + scale * ((sxy - down(sxy)) - sxx + (sxz - below(sxz)) + fx)
                planes.append([sxy, sxz, x])
            elif side == 2:
                x = vx + scale * ((up(sxx) - sxx) + sxy + (sxz - below(sxz)) + fx)
                z = vz + scale * ((sxz - down(sxz)) + syz + (above(szz) - szz) + fz)
                planes.append([syy, x, z])
            else:
                y = vy + scale * ((sxy - down(sxy)) - syy + (syz - below(syz)) + fy)
                planes.append([sxy, syz, y])
        return planes

    def completed(turn):
        dens = [received(0, side, len(STRESS_FACES[side])) for side in range(4)]
        far_syy, far_sxx = corner_in[turn, 0, 0:1], corner_in[turn, 0, 1:2]
        far_syz, far_sxz, far_sxy = corner_in[turn, 1, 0:1], corner_in[turn, 2, 0:1], corner_in[turn, 3, 0:1]
        high_x = (
            received(turn, 0, 1) + dens[0] * (on_row(far_syy, cy - 1, cy) - edge(state.at[6], 1)),
            received(turn, 0, 2) - dens[0] * (on_row(far_syz, 0, cy) + edge(state.at[7], 1)),
        )
        low_x = (received(turn, 1, 2) + dens[1] * (edge(state.at[3], 0) - on_row(far_sxy, 0, cy)),)
        high_y = (
            received(turn, 2, 1) + dens[2] * (on_row(far_sxx, cx - 1, cx) - edge(state.at[6], 3)),
            received(turn, 2, 2) - dens[2] * (on_row(far_sxz, 0, cx) + edge(state.at[8], 3)),
        )
        low_y = (received(turn, 3, 2) + dens[3] * (edge(state.at[4], 2) - on_row(far_sxy, 0, cx)),)
        return high_x, low_x, high_y, low_y

    def forward(step, f):
        return fwd_v[step, f].astype(jnp.float32).reshape(area, cz)

    cell = lax.broadcasted_iota(jnp.int32, (area, owned), 0).astype(jnp.float32)

    def sources():
        return [rows_out.at[0]] + [rows_in.at[d - 1] for d in range(1, n_sy)]

    def force(k):
        spread_out = sum(
            jnp.where(cell == rows[comps:comps + 1, :owned], rows[k:k + 1, :owned], 0.0) for rows in sources()
        )
        at_cell = jnp.sum(spread_out, axis=1, keepdims=True)
        return jnp.where(first_z, at_cell, 0.0)

    for d in range(1, n_sy):
        rows_copy(d).wait_recv()

    for c in range(3):
        forces[c] = force(c)
    first_counts = [len(faces) + 1 for faces in STRESS_FACES]
    velocity_counts = [len(faces) for faces in VELOCITY_FACES]
    late_counts = (3, 3, 3, 3)

    for step in range(steps):
        last = step == steps - 1
        turn = 0 if step == 0 else step + 1
        receive_faces(turn, first_counts if step == 0 else late_counts)
        if step > 0:
            receive_corners(turn)
            beside = completed(turn)
        sxx, syy, szz, sxy, sxz, syz = [state[3 + c] for c in range(6)]
        low_sxy, low_sxz = received(turn, 1, 0), received(turn, 1, 1)
        near_sxy, near_syz = received(turn, 3, 0), received(turn, 3, 1)
        accel_x = (next_x(sxx, received(turn, 0, 0)) - sxx) + (sxy - prev_y(sxy, near_sxy)) + (sxz - below(sxz))
        accel_y = (sxy - prev_x(sxy, low_sxy)) + (next_y(syy, received(turn, 2, 0)) - syy) + (syz - below(syz))
        accel_z = (sxz - prev_x(sxz, low_sxz)) + (syz - prev_y(syz, near_syz)) + (above(szz) - szz)
        scale = DT * dens_v[...]
        change = [scale * (a + forces[3 * step + c]) for c, a in enumerate((accel_x, accel_y, accel_z))]
        for c in range(3):
            state[c] = state[c] + change[c]
        if step == 0:
            send_faces(1, [[edge(state.at[f], side) for f in VELOCITY_FACES[side]] for side in range(4)])
            for k in range(3, comps):
                forces[k] = force(k)

        rho = sum(forward(step, c) * change[c] for c in range(3))
        total[0] = rho if step == 0 else total[0] + rho
        if last:
            for d in range(1, n_ev):
                kern_copy(d, 0, 1, 0).start()
        strain = [forward(step, 3 + c) for c in range(6)]

        if last:
            store(0, 3, 0).start()
        if step == 0:
            receive_faces(1, velocity_counts)
            beside = [[received(1, side, i) for i in range(velocity_counts[side])] for side in range(4)]
        high_x, low_x, high_y, low_y = beside
        vx, vy, vz = [state[c] for c in range(3)]
        exx = vx - prev_x(vx, low_x[0])
        eyy = vy - prev_y(vy, low_y[0])
        ezz = vz - below(vz)
        exy = 0.5 * ((next_y(vx, high_y[0]) - vx) + (next_x(vy, high_x[0]) - vy))
        exz = 0.5 * ((above(vx) - vx) + (next_x(vz, high_x[1]) - vz))
        eyz = 0.5 * ((above(vy) - vy) + (next_y(vz, high_y[1]) - vz))
        rates = (exx, eyy, ezz, exy, exz, eyz)
        trace = exx + eyy + ezz

        def update_stress():
            mu = (DT * 2.0) * shear_v[...]
            common = DT * lame_v[...] * trace
            for c in range(6):
                moved = mu * rates[c]
                state[3 + c] = state[3 + c] + (moved + common if c < 3 else moved)

        def update_kernels():
            lam = DT * (strain[0] + strain[1] + strain[2]) * trace
            diagonal = strain[0] * exx + strain[1] * eyy + strain[2] * ezz
            others = strain[3] * exy + strain[4] * exz + strain[5] * eyz
            she = (DT * 2.0) * (diagonal + 2.0 * others)
            total[1] = lam if step == 0 else total[1] + lam
            total[2] = she if step == 0 else total[2] + she

        if last:
            update_kernels()
            for d in range(1, n_ev):
                kern_copy(d, 1, 2, 1).start()
            update_stress()
            store(3, 6, 1).start()
        else:
            update_stress()
            send_faces(step + 2, advanced(step + 1))
            send_corners(step + 2)
            update_kernels()

    for turn in range(turns):
        sent = first_counts if turn == 0 else velocity_counts if turn == 1 else late_counts
        for side in range(4):
            @pl.when(goes[side])
            def _(turn=turn, side=side, count=sent[side]):
                face_copy(turn, side, count).wait_send()
        if turn > 1:
            for g in range(4):
                @pl.when(corner_goes[g])
                def _(turn=turn, g=g):
                    corner_copy(turn, g).wait_send()
    for d in range(1, n_sy):
        rows_copy(d).wait_send()
    for d in range(1, n_ev):
        kern_copy(d, 0, 1, 0).wait()
        kern_copy(d, 1, 2, 1).wait()
    for c in range(3):
        value = total[c]
        for d in range(1, n_ev):
            value = value + kern_in[d - 1, c]
        total[c] = value
    finish = pltpu.make_async_copy(total, total_out, store_sem.at[2])
    finish.start()
    store(0, 3, 0).wait()
    store(3, 6, 1).wait()
    finish.wait()


def on_device(
    sizes,
    adjoint_state,
    forward_state,
    inv_density,
    lame_lambda,
    shear_modulus,
    station_block,
    station_cell,
    station_trace,
    source_count,
):
    n_sx, n_sy, n_ev = sizes
    fields, cx, cy, cz = adjoint_state.shape[1:]
    steps = forward_state.shape[1]
    owned = station_cell.shape[1]
    area, wide = cx * cy, max(cx, cy)
    hbm = pl.BlockSpec(memory_space=pl.ANY)
    lines = -(-(3 * steps + 1) // 8) * 8
    f32, i32 = jnp.float32, jnp.int32
    state, kernels = pl.pallas_call(
        functools.partial(kernel, n_sx, n_sy, n_ev, cx, cy, cz, steps, owned),
        out_shape=(
            jax.ShapeDtypeStruct((fields, area, cz), f32),
            jax.ShapeDtypeStruct((3, area, cz), f32),
        ),
        in_specs=[hbm] * 8 + [pl.BlockSpec(memory_space=pltpu.SMEM)],
        out_specs=(hbm, hbm),
        scratch_shapes=[
            pltpu.VMEM((fields, area, cz), f32),
            pltpu.VMEM((3, area, cz), f32),
            pltpu.VMEM((3 * steps, area, cz), f32),
            pltpu.VMEM((steps, fields, cx, cy, cz), jnp.bfloat16),
            pltpu.VMEM((area, cz), f32),
            pltpu.VMEM((area, cz), f32),
            pltpu.VMEM((area, cz), f32),
            pltpu.VMEM((1, 1, owned), i32),
            pltpu.VMEM((1, owned), i32),
            pltpu.VMEM((3 * steps, 1, owned), f32),
            pltpu.VMEM((steps + 1, 4, 3, wide, cz), f32),
            pltpu.VMEM((steps + 1, 4, 3, wide, cz), f32),
            pltpu.VMEM((steps + 1, 4, 8, cz), f32),
            pltpu.VMEM((steps + 1, 4, 8, cz), f32),
            pltpu.VMEM((n_sy, lines, 128), f32),
            pltpu.VMEM((max(1, n_sy - 1), lines, 128), f32),
            pltpu.VMEM((max(1, n_ev - 1), 3, area, cz), f32),
            pltpu.SemaphoreType.DMA((8,)),
            pltpu.SemaphoreType.DMA((3,)),
            pltpu.SemaphoreType.DMA((steps + 1, 4)),
            pltpu.SemaphoreType.DMA((steps + 1, 4)),
            pltpu.SemaphoreType.DMA((steps + 1, 4)),
            pltpu.SemaphoreType.DMA((steps + 1, 4)),
            pltpu.SemaphoreType.DMA((max(1, n_sy - 1),)),
            pltpu.SemaphoreType.DMA((max(1, n_sy - 1),)),
            pltpu.SemaphoreType.DMA((max(1, n_ev - 1), 2)),
            pltpu.SemaphoreType.DMA((max(1, n_ev - 1), 2)),
        ],
        compiler_params=pltpu.CompilerParams(
            collective_id=0, has_side_effects=True, vmem_limit_bytes=60 * 1024 * 1024
        ),
    )(
        adjoint_state.reshape(fields, area, cz),
        forward_state[0],
        inv_density.reshape(area, cz),
        lame_lambda.reshape(area, cz),
        shear_modulus.reshape(area, cz),
        station_block.transpose(0, 2, 1),
        station_cell,
        station_trace.transpose(2, 0, 1),
        source_count,
    )
    return state.reshape(1, fields, cx, cy, cz), kernels.reshape(3, cx, cy, cz)


def solution(mesh):
    sizes = tuple(mesh.shape[name] for name in ("sx", "sy", "ev"))
    return jax.shard_map(
        functools.partial(on_device, sizes),
        mesh=mesh,
        in_specs=(
            P("ev", None, "sx", "sy", None),
            P("ev", None, None, "sx", "sy", None),
            P("sx", "sy", None),
            P("sx", "sy", None),
            P("sx", "sy", None),
            P("ev", ("sx", "sy"), None),
            P("ev", ("sx", "sy")),
            P("ev", ("sx", "sy"), None),
            P("ev", ("sx", "sy")),
        ),
        out_specs=(P("ev", None, "sx", "sy", None), P(None, "sx", "sy", None)),
        check_vma=False,
    )
```

time: 34.8 us -> 26.2 us (0.75)
  local copies, waits for them, and re-layouts: 7 us -> 2.37 us
  Pallas kernels: 26 us -> 22.3 us
    unnamed x15 -> x4, local copies, waits for them, and re-layouts: 6.27 us -> 2.37 us
    pallas_call x1, Pallas kernels: 26 us -> 22.3 us  [on_device(): pl.pallas_call(functools.partial(kernel, n_sx, n_sy, n_ev, cx, cy, cz, st...]
    squeeze x1 -> x0, local copies, waits for them, and re-layouts: 0.74 us -> none  [on_device(): station_block[0]]
where the time goes in v2:
time: 26.2 us; the launch traced here: 26 us
  Pallas kernels  22.3 us (85%)
  local copies, waits for them, and re-layouts  2.37 us (9%)
  between operations  1.3 us (5%)
    pallas_call x1, Pallas kernels, on_device(): pl.pallas_call(functools.partial(kernel, n_sx, n_sy, n_ev, cx, cy, cz, st...  22.3 us
    unnamed x4, local copies, waits for them, and re-layouts  2.37 us

profile of v2, /device:TPU:0, one launch (start us, length us, event | category | flops | bytes accessed | tf_op | source)
XLA Modules:
  0.0 26.0 jit_solution(6206951362199625290)
XLA Ops:
  1.3 22.3 %shard_map.104 = (f32[9,64,128]{2,1,0:T(8,128)}, f32[3,64,128]{2,1,0:T(8,128)}) custom-call(f32[9,64,128]{2,1,0:T(8,128)} %bitcast.10, bf16[3,9,8,8,128]{4,3,2,1,0:T(8,128)(2,1)} %bitcast.9, f32[64,128]{1,0:T(8,128)} %bitcast.13, f32[64,128]{1,0:T(8,128)} %bitcast.14, f32[64,128]{1,0:T(8,128)} %bitcast.15, s32[1,1,32]{2,1,0:T(1,128)} %bitcast.17, ...), custom_call_target="tpu_custom_call" | custom-call | tf_op jit(solution)/shard_map/pallas_call | solution.py:401
  23.6 0.0 copy-start
  23.6 1.7 %copy.14 = f32[1,9,8,8,128]{4,3,2,1,0:T(8,128)} copy(f32[1,9,8,8,128]{4,3,2,1,0:T(8,128)} %bitcast.11) | data formatting | bytes 589824
  25.3 0.0 copy-done
  25.4 0.6 %copy.15 = f32[3,8,8,128]{3,2,1,0:T(8,128)} copy(f32[3,8,8,128]{3,2,1,0:T(8,128)S(1)} %bitcast.12) | data formatting | bytes 196608
Async XLA Ops:
  23.6 1.7 %copy-start = (f32[3,64,128]{2,1,0:T(8,128)S(1)}, f32[3,64,128]{2,1,0:T(8,128)}, u32[]{:S(2)}) copy-start(f32[3,64,128]{2,1,0:T(8,128)} %get-tuple-element.5) | copy-start | bytes 294916

commit v3 on v2

--- a/solution.py
+++ b/solution.py
@@ -10,17 +10,14 @@
 DT = 0.35
 MESH = pl.DeviceIdType.MESH
 
-STRESS_FACES = ((3,), (6, 7), (4,), (6, 8))
-VELOCITY_FACES = ((1, 2), (0,), (0, 2), (1,))
-
 
 def kernel(
     n_sx, n_sy, n_ev, cx, cy, cz, steps, owned,
     adj, fwd, inv_density, lame, shear, blocks, cells, traces, counts,
-    state_out, total_out,
-    state, total, forces, fwd_v, dens_v, lame_v, shear_v, blocks_v, cells_v, traces_v,
+    state, total,
+    forces, fwd_v, dens_v, lame_v, shear_v, blocks_v, cells_v, traces_v,
     plane_out, plane_in, corner_out, corner_in, rows_out, rows_in, kern_in,
-    load_sem, store_sem, face_send, face_recv, corner_send, corner_recv, rows_send, rows_recv, kern_send, kern_recv,
+    load_sem, face_send, face_recv, corner_send, corner_recv, rows_send, rows_recv, kern_send, kern_recv,
 ):
     ix, iy, ie = lax.axis_index("sx"), lax.axis_index("sy"), lax.axis_index("ev")
     area = cx * cy
@@ -30,9 +27,6 @@
         (inv_density, dens_v), (adj, state), (fwd, fwd_v), (lame, lame_v), (shear, shear_v),
     ]
     loads = [pltpu.make_async_copy(a, b, load_sem.at[i]) for i, (a, b) in enumerate(pairs)]
-    for load in loads:
-        load.start()
-
     goes = (ix > 0, ix < n_sx - 1, iy > 0, iy < n_sy - 1)
     comes = (ix < n_sx - 1, ix > 0, iy < n_sy - 1, iy > 0)
     targets = ({"sx": ix - 1}, {"sx": ix + 1}, {"sy": iy - 1}, {"sy": iy + 1})
@@ -40,47 +34,46 @@
     corner_goes = [jnp.logical_and(goes[a], goes[b]) for a, b in corners]
     corner_comes = [jnp.logical_and(comes[a], comes[b]) for a, b in corners]
     corner_targets = [{**targets[a], **targets[b]} for a, b in corners]
-    turns = steps + 1
 
     barrier = pltpu.get_barrier_semaphore()
     for side in (0, 1):
         @pl.when(goes[side])
         def _(side=side):
-            pl.semaphore_signal(barrier, inc=1, device_id=targets[side], device_id_type=MESH)
-    for g in range(4):
-        @pl.when(corner_goes[g])
-        def _(g=g):
-            pl.semaphore_signal(barrier, inc=1, device_id=corner_targets[g], device_id_type=MESH)
+            for y in range(n_sy):
+                where = {**targets[side], "sy": y}
+                pl.semaphore_signal(barrier, inc=1, device_id=where, device_id_type=MESH)
     for d in range(1, n_sy):
         pl.semaphore_signal(barrier, inc=1, device_id={"sy": lax.rem(iy + d, n_sy)}, device_id_type=MESH)
     for d in range(1, n_ev):
         pl.semaphore_signal(barrier, inc=1, device_id={"ev": lax.rem(ie + d, n_ev)}, device_id_type=MESH)
 
+    for load in loads:
+        load.start()
+
     for side in range(4):
         @pl.when(jnp.logical_not(comes[side]))
         def _(side=side):
-            plane_in[:, side] = jnp.zeros((turns, 3, max(cx, cy), cz), jnp.float32)
+            plane_in[:, side] = jnp.zeros((steps, 4, max(cx, cy), cz), jnp.float32)
     for g in range(4):
         @pl.when(jnp.logical_not(corner_comes[g]))
         def _(g=g):
-            corner_in[:, g] = jnp.zeros((turns, 8, cz), jnp.float32)
+            corner_in[:, g] = jnp.zeros((steps, 8, cz), jnp.float32)
+    for side in (0, 1):
+        @pl.when(jnp.logical_not(comes[side]))
+        def _(side=side):
+            rows_in[1 + side] = jnp.zeros(rows_in.shape[1:], jnp.float32)
     corner_out[...] = jnp.zeros(corner_out.shape, jnp.float32)
 
     for load in loads[:3]:
         load.wait()
     comps = 3 * steps
     live = lax.broadcasted_iota(jnp.int32, (1, owned), 1) < counts[0, 0]
-    for d in range(n_sy):
-        goal = lax.rem(iy + d, n_sy)
-        keep = jnp.logical_and(live, blocks_v[0] == goal)
-        for k in range(comps):
-            rows_out[d, k:k + 1, :owned] = jnp.where(keep, traces_v[k], 0.0)
-        rows_out[d, comps:comps + 1, :owned] = cells_v[...].astype(jnp.float32)
-
-    amount = (n_sy - 1) + (n_ev - 1) + (ix > 0).astype(jnp.int32) + (ix < n_sx - 1).astype(jnp.int32)
-    for g in range(4):
-        amount = amount + corner_goes[g].astype(jnp.int32)
-    pl.semaphore_wait(barrier, amount)
+    for k in range(comps):
+        rows_out[k:k + 1, :owned] = jnp.where(live, traces_v[k], 0.0)
+    rows_out[comps:comps + 1, :owned] = (blocks_v[0] * area + cells_v[...]).astype(jnp.float32)
+
+    across = n_sy * ((ix > 0).astype(jnp.int32) + (ix < n_sx - 1).astype(jnp.int32))
+    pl.semaphore_wait(barrier, (n_sy - 1) + (n_ev - 1) + across)
 
     def face_copy(turn, side, count):
         return pltpu.make_async_remote_copy(
@@ -139,19 +132,16 @@
             def _(g=g):
                 corner_copy(turn, g).wait_recv()
 
-    def rows_copy(d):
+    def rows_copy(line, d):
+        where = {"sy": lax.rem(iy + d, n_sy)}
         return pltpu.make_async_remote_copy(
-            src_ref=rows_out.at[d],
-            dst_ref=rows_in.at[d - 1],
-            send_sem=rows_send.at[d - 1],
-            recv_sem=rows_recv.at[d - 1],
-            device_id={"sy": lax.rem(iy + d, n_sy)},
+            src_ref=rows_out,
+            dst_ref=rows_in.at[line, d],
+            send_sem=rows_send.at[line, d],
+            recv_sem=rows_recv.at[line, d],
+            device_id={**targets[line - 1], **where} if line else where,
             device_id_type=MESH,
         )
-
-    def store(first, count, part):
-        fields = pl.ds(first, count)
-        return pltpu.make_async_copy(state.at[fields], state_out.at[fields], store_sem.at[part])
 
     def kern_copy(d, first, count, part):
         return pltpu.make_async_remote_copy(
@@ -163,17 +153,6 @@
             device_id_type=MESH,
         )
 
-    loads[3].wait()
-    loads[4].wait()
-    send_faces(
-        0,
-        [[edge(state.at[f], side) for f in STRESS_FACES[side]] + [DT * edge(dens_v, side)] for side in range(4)],
-    )
-    for d in range(1, n_sy):
-        rows_copy(d).start()
-    for load in loads[5:]:
-        load.wait()
-
     lane = lax.broadcasted_iota(jnp.int32, (area, cz), 1)
     y_at = lax.rem(lax.broadcasted_iota(jnp.int32, (area, cz), 0), cy)
     first_z, last_z = lane == 0, lane == cz - 1
@@ -216,11 +195,11 @@
     def received(turn, side, i):
         return plane_in[turn, side, i, :cy if side < 2 else cx]
 
-    def advanced(step):
+    def advanced(step, with_force=True):
         planes = []
         for side in range(4):
             vx, vy, vz, sxx, syy, szz, sxy, sxz, syz = [edge(state.at[f], side) for f in range(9)]
-            fx, fy, fz = [edge(forces.at[3 * step + c], side) for c in range(3)]
+            fx, fy, fz = [edge(forces.at[3 * step + c], side) if with_force else 0.0 for c in range(3)]
             scale = DT * edge(dens_v, side)
             if side == 0:
                 y = vy + scale * (sxy + (up(syy) - syy) + (syz - below(syz)) + fy)
@@ -239,7 +218,7 @@
         return planes
 
     def completed(turn):
-        dens = [received(0, side, len(STRESS_FACES[side])) for side in range(4)]
+        dens = [received(0, side, 3) for side in range(4)]
         far_syy, far_sxx = corner_in[turn, 0, 0:1], corner_in[turn, 0, 1:2]
         far_syz, far_sxz, far_sxy = corner_in[turn, 1, 0:1], corner_in[turn, 2, 0:1], corner_in[turn, 3, 0:1]
         high_x = (
@@ -257,34 +236,55 @@
     def forward(step, f):
         return fwd_v[step, f].astype(jnp.float32).reshape(area, cz)
 
-    cell = lax.broadcasted_iota(jnp.int32, (area, owned), 0).astype(jnp.float32)
-
-    def sources():
-        return [rows_out.at[0]] + [rows_in.at[d - 1] for d in range(1, n_sy)]
-
-    def force(k):
-        spread_out = sum(
-            jnp.where(cell == rows[comps:comps + 1, :owned], rows[k:k + 1, :owned], 0.0) for rows in sources()
-        )
-        at_cell = jnp.sum(spread_out, axis=1, keepdims=True)
-        return jnp.where(first_z, at_cell, 0.0)
-
+    loads[3].wait()
+    loads[4].wait()
+    start = [planes + [DT * edge(dens_v, side)] for side, planes in enumerate(advanced(0, False))]
+    send_faces(0, start)
+    send_corners(0)
     for d in range(1, n_sy):
-        rows_copy(d).wait_recv()
-
+        rows_copy(0, d).start()
+    for side in (0, 1):
+        @pl.when(goes[side])
+        def _(side=side):
+            for d in range(n_sy):
+                rows_copy(1 + side, d).start()
+    for load in loads[5:]:
+        load.wait()
+
+    def force(k, sources, first, stride, count):
+        code = (first + stride * lax.broadcasted_iota(jnp.int32, (count, owned), 0)).astype(jnp.float32)
+        found = sum(jnp.where(code == rows[comps:comps + 1, :owned], rows[k:k + 1, :owned], 0.0) for rows in sources)
+        return jnp.where(first_z[:count], jnp.sum(found, axis=1, keepdims=True), 0.0)
+
+    for d in range(1, n_sy):
+        rows_copy(0, d).wait_recv()
+    for side in (0, 1):
+        @pl.when(comes[side])
+        def _(side=side):
+            for d in range(n_sy):
+                rows_copy(1 + side, d).wait_recv()
+    here = [rows_out] + [rows_in.at[0, d] for d in range(1, n_sy)]
+    higher, lower = [[rows_in.at[line, d] for d in range(n_sy)] for line in (1, 2)]
+    base = iy * area
     for c in range(3):
-        forces[c] = force(c)
-    first_counts = [len(faces) + 1 for faces in STRESS_FACES]
-    velocity_counts = [len(faces) for faces in VELOCITY_FACES]
-    late_counts = (3, 3, 3, 3)
+        forces[c] = force(c, here, base, 1, area)
+    beside_force = (
+        [force(c, higher, base, 1, cy) for c in (1, 2)],
+        [force(0, lower, base + area - cy, 1, cy)],
+        [force(c, here, base + area, cy, cx) for c in (0, 2)],
+        [force(1, here, base - area + cy - 1, cy, cx)],
+    )
 
     for step in range(steps):
         last = step == steps - 1
-        turn = 0 if step == 0 else step + 1
-        receive_faces(turn, first_counts if step == 0 else late_counts)
-        if step > 0:
-            receive_corners(turn)
-            beside = completed(turn)
+        receive_faces(step, [4 if step == 0 else 3] * 4)
+        receive_corners(step)
+        turn = step
+        beside = completed(step)
+        if step == 0:
+            beside = [
+                [v + received(0, side, 3) * f for v, f in zip(beside[side], beside_force[side])] for side in range(4)
+            ]
         sxx, syy, szz, sxy, sxz, syz = [state[3 + c] for c in range(6)]
         low_sxy, low_sxz = received(turn, 1, 0), received(turn, 1, 1)
         near_sxy, near_syz = received(turn, 3, 0), received(turn, 3, 1)
@@ -296,9 +296,8 @@
         for c in range(3):
             state[c] = state[c] + change[c]
         if step == 0:
-            send_faces(1, [[edge(state.at[f], side) for f in VELOCITY_FACES[side]] for side in range(4)])
             for k in range(3, comps):
-                forces[k] = force(k)
+                forces[k] = force(k, here, base, 1, area)
 
         rho = sum(forward(step, c) * change[c] for c in range(3))
         total[0] = rho if step == 0 else total[0] + rho
@@ -307,11 +306,6 @@
                 kern_copy(d, 0, 1, 0).start()
         strain = [forward(step, 3 + c) for c in range(6)]
 
-        if last:
-            store(0, 3, 0).start()
-        if step == 0:
-            receive_faces(1, velocity_counts)
-            beside = [[received(1, side, i) for i in range(velocity_counts[side])] for side in range(4)]
         high_x, low_x, high_y, low_y = beside
         vx, vy, vz = [state[c] for c in range(3)]
         exx = vx - prev_x(vx, low_x[0])
@@ -332,50 +326,49 @@
 
         def update_kernels():
             lam = DT * (strain[0] + strain[1] + strain[2]) * trace
+            total[1] = lam if step == 0 else total[1] + lam
+            if last:
+                for d in range(1, n_ev):
+                    kern_copy(d, 1, 1, 1).start()
             diagonal = strain[0] * exx + strain[1] * eyy + strain[2] * ezz
             others = strain[3] * exy + strain[4] * exz + strain[5] * eyz
             she = (DT * 2.0) * (diagonal + 2.0 * others)
-            total[1] = lam if step == 0 else total[1] + lam
             total[2] = she if step == 0 else total[2] + she
 
         if last:
             update_kernels()
             for d in range(1, n_ev):
-                kern_copy(d, 1, 2, 1).start()
+                kern_copy(d, 2, 1, 2).start()
             update_stress()
-            store(3, 6, 1).start()
         else:
             update_stress()
-            send_faces(step + 2, advanced(step + 1))
-            send_corners(step + 2)
+            send_faces(step + 1, advanced(step + 1))
+            send_corners(step + 1)
             update_kernels()
 
-    for turn in range(turns):
-        sent = first_counts if turn == 0 else velocity_counts if turn == 1 else late_counts
+    for turn in range(steps):
         for side in range(4):
             @pl.when(goes[side])
-            def _(turn=turn, side=side, count=sent[side]):
-                face_copy(turn, side, count).wait_send()
-        if turn > 1:
-            for g in range(4):
-                @pl.when(corner_goes[g])
-                def _(turn=turn, g=g):
-                    corner_copy(turn, g).wait_send()
+            def _(turn=turn, side=side):
+                face_copy(turn, side, 4 if turn == 0 else 3).wait_send()
+        for g in range(4):
+            @pl.when(corner_goes[g])
+            def _(turn=turn, g=g):
+                corner_copy(turn, g).wait_send()
     for d in range(1, n_sy):
-        rows_copy(d).wait_send()
-    for d in range(1, n_ev):
-        kern_copy(d, 0, 1, 0).wait()
-        kern_copy(d, 1, 2, 1).wait()
+        rows_copy(0, d).wait_send()
+    for side in (0, 1):
+        @pl.when(goes[side])
+        def _(side=side):
+            for d in range(n_sy):
+                rows_copy(1 + side, d).wait_send()
     for c in range(3):
+        for d in range(1, n_ev):
+            kern_copy(d, c, 1, c).wait()
         value = total[c]
         for d in range(1, n_ev):
             value = value + kern_in[d - 1, c]
         total[c] = value
-    finish = pltpu.make_async_copy(total, total_out, store_sem.at[2])
-    finish.start()
-    store(0, 3, 0).wait()
-    store(3, 6, 1).wait()
-    finish.wait()
 
 
 def on_device(
@@ -395,7 +388,7 @@
     steps = forward_state.shape[1]
     owned = station_cell.shape[1]
     area, wide = cx * cy, max(cx, cy)
-    hbm = pl.BlockSpec(memory_space=pl.ANY)
+    hbm = pl.BlockSpec(memory_space=pltpu.HBM)
     lines = -(-(3 * steps + 1) // 8) * 8
     f32, i32 = jnp.float32, jnp.int32
     state, kernels = pl.pallas_call(
@@ -405,10 +398,8 @@
             jax.ShapeDtypeStruct((3, area, cz), f32),
         ),
         in_specs=[hbm] * 8 + [pl.BlockSpec(memory_space=pltpu.SMEM)],
-        out_specs=(hbm, hbm),
+        out_specs=[pl.BlockSpec(memory_space=pltpu.VMEM)] * 2,
         scratch_shapes=[
-            pltpu.VMEM((fields, area, cz), f32),
-            pltpu.VMEM((3, area, cz), f32),
             pltpu.VMEM((3 * steps, area, cz), f32),
             pltpu.VMEM((steps, fields, cx, cy, cz), jnp.bfloat16),
             pltpu.VMEM((area, cz), f32),
@@ -417,36 +408,40 @@
             pltpu.VMEM((1, 1, owned), i32),
             pltpu.VMEM((1, owned), i32),
             pltpu.VMEM((3 * steps, 1, owned), f32),
-            pltpu.VMEM((steps + 1, 4, 3, wide, cz), f32),
-            pltpu.VMEM((steps + 1, 4, 3, wide, cz), f32),
-            pltpu.VMEM((steps + 1, 4, 8, cz), f32),
-            pltpu.VMEM((steps + 1, 4, 8, cz), f32),
-            pltpu.VMEM((n_sy, lines, 128), f32),
-            pltpu.VMEM((max(1, n_sy - 1), lines, 128), f32),
+            pltpu.VMEM((steps, 4, 4, wide, cz), f32),
+            pltpu.VMEM((steps, 4, 4, wide, cz), f32),
+            pltpu.VMEM((steps, 4, 8, cz), f32),
+            pltpu.VMEM((steps, 4, 8, cz), f32),
+            pltpu.VMEM((lines, 128), f32),
+            pltpu.VMEM((3, n_sy, lines, 128), f32),
             pltpu.VMEM((max(1, n_ev - 1), 3, area, cz), f32),
             pltpu.SemaphoreType.DMA((8,)),
-            pltpu.SemaphoreType.DMA((3,)),
-            pltpu.SemaphoreType.DMA((steps + 1, 4)),
-            pltpu.SemaphoreType.DMA((steps + 1, 4)),
-            pltpu.SemaphoreType.DMA((steps + 1, 4)),
-            pltpu.SemaphoreType.DMA((steps + 1, 4)),
-            pltpu.SemaphoreType.DMA((max(1, n_sy - 1),)),
-            pltpu.SemaphoreType.DMA((max(1, n_sy - 1),)),
-            pltpu.SemaphoreType.DMA((max(1, n_ev - 1), 2)),
-            pltpu.SemaphoreType.DMA((max(1, n_ev - 1), 2)),
+            pltpu.SemaphoreType.DMA((steps, 4)),
+            pltpu.SemaphoreType.DMA((steps, 4)),
+            pltpu.SemaphoreType.DMA((steps, 4)),
+            pltpu.SemaphoreType.DMA((steps, 4)),
+            pltpu.SemaphoreType.DMA((3, n_sy)),
+            pltpu.SemaphoreType.DMA((3, n_sy)),
+            pltpu.SemaphoreType.DMA((max(1, n_ev - 1), 3)),
+            pltpu.SemaphoreType.DMA((max(1, n_ev - 1), 3)),
         ],
         compiler_params=pltpu.CompilerParams(
-            collective_id=0, has_side_effects=True, vmem_limit_bytes=60 * 1024 * 1024
+            collective_id=0, has_side_effects=True, vmem_limit_bytes=24 * 1024 * 1024
         ),
     )(
-        adjoint_state.reshape(fields, area, cz),
-        forward_state[0],
-        inv_density.reshape(area, cz),
-        lame_lambda.reshape(area, cz),
-        shear_modulus.reshape(area, cz),
-        station_block.transpose(0, 2, 1),
-        station_cell,
-        station_trace.transpose(2, 0, 1),
+        *(
+            pltpu.with_memory_space_constraint(x, pltpu.HBM)
+            for x in (
+                adjoint_state.reshape(fields, area, cz),
+                forward_state[0],
+                inv_density.reshape(area, cz),
+                lame_lambda.reshape(area, cz),
+                shear_modulus.reshape(area, cz),
+                station_block.transpose(0, 2, 1),
+                station_cell,
+                station_trace.transpose(2, 0, 1),
+            )
+        ),
         source_count,
     )
     return state.reshape(1, fields, cx, cy, cz), kernels.reshape(3, cx, cy, cz)

time: 26.2 us -> 23 us (0.88)
  Pallas kernels: 22.3 us -> 20.1 us
  local copies, waits for them, and re-layouts: 2.37 us -> 1.36 us
    pallas_call x1, Pallas kernels: 22.3 us -> 20.1 us  [on_device(): pl.pallas_call(functools.partial(kernel, n_sx, n_sy, n_ev, cx, cy, cz, st...]
    unnamed x4 -> x2, local copies, waits for them, and re-layouts: 2.37 us -> 1.36 us
where the time goes in v3:
time: 23 us; the launch traced here: 22.8 us
  Pallas kernels  20.1 us (87%)
  local copies, waits for them, and re-layouts  1.36 us (6%)
  between operations  1.29 us (6%)
    pallas_call x1, Pallas kernels, on_device(): pl.pallas_call(functools.partial(kernel, n_sx, n_sy, n_ev, cx, cy, cz, st...  20.1 us
    unnamed x2, local copies, waits for them, and re-layouts  1.36 us

profile of v3, /device:TPU:0, one launch (start us, length us, event | category | flops | bytes accessed | tf_op | source)
XLA Modules:
  0.0 22.8 jit_solution(14882241989623466885)
XLA Ops:
  1.3 20.1 %shard_map.104 = (f32[9,64,128]{2,1,0:T(8,128)S(1)}, f32[3,64,128]{2,1,0:T(8,128)S(1)}) custom-call(f32[9,64,128]{2,1,0:T(8,128)} %bitcast.12, bf16[3,9,8,8,128]{4,3,2,1,0:T(8,128)(2,1)} %bitcast.11, f32[64,128]{1,0:T(8,128)} %bitcast.13, f32[64,128]{1,0:T(8,128)} %bitcast.14, f32[64,128]{1,0:T(8,128)} %bitcast.15, s32[1,1,32]{2,1,0:T(1,128)} %bitcast.17, ...), custom_call_target="tpu_custom_call" | custom-call | tf_op jit(solution)/shard_map/pallas_call | solution.py:394
  21.4 0.7 %copy.14 = f32[1,9,8,8,128]{4,3,2,1,0:T(8,128)} copy(f32[1,9,8,8,128]{4,3,2,1,0:T(8,128)S(1)} %bitcast.9) | data formatting | bytes 589824
  22.1 0.6 %copy.15 = f32[3,8,8,128]{3,2,1,0:T(8,128)} copy(f32[3,8,8,128]{3,2,1,0:T(8,128)S(1)} %bitcast.10) | data formatting | bytes 196608
